TPU v7x, 512 devices: a whole 4x8x8 slice. The times are simulated.
512 devices in a mesh: clu: 128 (over z, y, core), sub: 4 (over x).
Axes of the slice: x: 4, y: 8, z: 8, core: 2. Of those that a mesh axis runs over, the one named last changes fastest.
Arguments:
- p_dir: bfloat16 [256, 256, 512], P('clu', None, 'sub'), may hold values from -200 to 200
- q_dir: bfloat16 [256, 256, 512], P('clu', None, 'sub'), may hold values from -200 to 200
- mass: float32 [256, 512], P('clu', 'sub'), may hold values from 0.5 to 2
- nearby_tile_blocks: bfloat16 [256, 16, 512, 512], P('clu', None, None, 'sub'), may hold values from -0.09375 to 0.09375
- near_ids: int32 [256, 16], P('clu'), may hold values from 0 to 255, as said below
- near_count: int32 [256], P('clu'), may hold values from 4 to 16, as said below
- col_basis: bfloat16 [256, 64, 512], P('clu', None, 'sub'), may hold values from -0.25 to 0.25
- row_basis: bfloat16 [256, 64, 512], P('clu', None, 'sub'), may hold values from -0.75 to 0.75
- col_transfer: bfloat16 [256, 64, 64], P('clu'), may hold values from -0.75 to 0.75
- row_transfer: bfloat16 [256, 64, 64], P('clu'), may hold values from -0.75 to 0.75
- couplings: bfloat16 [128, 8, 64, 64], P('clu', 'sub'), may hold values from -0.25 to 0.25
- far_ids: int32 [128, 8], P('clu', 'sub'), may hold values from 0 to 127, as said below
Outputs:
- v_next: float32 [256, 256, 512], P('clu', None, 'sub')
- w_next: float32 [256, 256, 512], P('clu', None, 'sub')
- delta: float32 [256], replicated
Inputs may be any that keep to these rules, and one draw needn't show every extreme that they name: `near_ids`: cluster c is kept with parent c // 2. Every slot names a cluster whose parent is within 3 of the cluster's own parent; slot 0 is the cluster itself; slots at or after near_count are padding and still obey the reach. Some slot reaches exactly 3 parents away. `near_count`: some cluster fills all 16 slots. `far_ids`: every slot of parent P names a parent within 6 of P; some slot reaches exactly 6.
All inputs are finite; a program needn't handle non-finite values.
Results may differ from a plain program's by a relative error of at most 0.00045.
Values may be sent and summed in bfloat16 or wider, within the bound.
A program may use at most 64 MiB of HBM per device.

v0:
```python
import jax
import jax.numpy as jnp
from jax import lax
from jax.sharding import PartitionSpec as P

NEAR_RADIUS = 3
FAR_REACH = 6


HIGH = lax.Precision.HIGHEST


def from_behind(block, axis, distance):
    devices = range(lax.axis_size(axis))
    route = [(i - distance, i) for i in devices if i - distance in devices]
    return lax.ppermute(block, axis, route)


def on_device(
    p_dir,
    q_dir,
    mass,
    nearby_tile_blocks,
    near_ids,
    near_count,
    col_basis,
    row_basis,
    col_transfer,
    row_transfer,
    couplings,
    far_ids,
):
    f32 = jnp.float32
    clusters, rhs_count, quarter = p_dir.shape
    slot_count = nearby_tile_blocks.shape[1]
    here = lax.axis_index("clu")
    pc_part = jnp.einsum("crn,ckn->crk", p_dir, col_basis, preferred_element_type=f32)
    qc_part = jnp.einsum("crn,ckn->crk", q_dir, row_basis, preferred_element_type=f32)
    pc_sum, qc_sum = lax.psum((pc_part, qc_part), "sub")
    pg_own = jnp.einsum("crk,ckl->rl", pc_sum, col_transfer.astype(f32), precision=HIGH)
    qg_own = jnp.einsum("crk,ckl->rl", qc_sum, row_transfer.astype(f32), precision=HIGH)
    far_here = far_ids[0]
    coup = couplings[0].astype(f32)
    parent_pieces = []
    for start_offset in range(-FAR_REACH, FAR_REACH + 1):
        if start_offset == 0:
            parent_pieces.append(pg_own[None])
        else:
            parent_pieces.append(from_behind(pg_own[None], "clu", -start_offset))
    parent_window = jnp.concatenate(parent_pieces, axis=0)
    picked = parent_window[far_here - (here - FAR_REACH)]
    ph_part = jnp.einsum("srl,skl->rk", picked, coup, precision=HIGH)
    far_terms = jnp.einsum("rk,skl->srl", qg_own, coup, precision=HIGH)
    far_span = 2 * FAR_REACH + 1
    far_slot = far_here - (here - FAR_REACH)
    far_onehot = (far_slot[None, :] == jnp.arange(far_span, dtype=jnp.int32)[:, None]).astype(f32)
    far_acc = jnp.einsum("ws,srl->wrl", far_onehot, far_terms, precision=HIGH)
    near_pieces = []
    for start_offset in range(-NEAR_RADIUS, NEAR_RADIUS + 1):
        if start_offset == 0:
            near_pieces.append(p_dir)
        else:
            near_pieces.append(from_behind(p_dir, "clu", -start_offset))
    near_window = jnp.concatenate(near_pieces, axis=0)
    near_span = (2 * NEAR_RADIUS + 1) * clusters
    local_idx = near_ids - (here - NEAR_RADIUS) * clusters
    live = jnp.arange(slot_count, dtype=jnp.int32)[None, :] < near_count[:, None]
    chosen = near_window[local_idx] * live[:, :, None, None].astype(jnp.bfloat16)
    pn_part = jnp.einsum("csmn,csrn->crm", nearby_tile_blocks, chosen, preferred_element_type=f32)
    pn_vec = lax.psum_scatter(pn_part, "sub", scatter_dimension=2, tiled=True)
    q_rows = lax.all_gather(q_dir, "sub", axis=2, tiled=True)
    back = jnp.einsum("csmn,crm->csrn", nearby_tile_blocks, q_rows, preferred_element_type=f32)
    back = back * live[:, :, None, None].astype(f32)
    near_onehot = (
        local_idx.reshape(-1)[None, :] == jnp.arange(near_span, dtype=jnp.int32)[:, None]
    ).astype(f32)
    near_acc = jnp.einsum(
        "wj,jrn->wrn",
        near_onehot,
        back.reshape(clusters * slot_count, rhs_count, quarter),
        precision=HIGH,
    )

    def near_block(start_offset):
        start = (start_offset + NEAR_RADIUS) * clusters
        return near_acc[start : start + clusters]

    def far_block(start_offset):
        return far_acc[start_offset + FAR_REACH][None]

    qn_vec = near_block(0)
    qh_part = far_acc[FAR_REACH]
    for start_offset in range(-FAR_REACH, FAR_REACH + 1):
        if start_offset == 0:
            continue
        if abs(start_offset) <= NEAR_RADIUS:
            got_near, got_far = from_behind(
                (near_block(start_offset), far_block(start_offset)), "clu", start_offset
            )
            qn_vec = qn_vec + got_near
        else:
            got_far = from_behind(far_block(start_offset), "clu", start_offset)
        qh_part = qh_part + got_far[0]
    ph_own, qh_own = lax.psum((ph_part, qh_part), "sub")
    down_p = jnp.einsum("rl,ckl->crk", ph_own, row_transfer.astype(f32), precision=HIGH)
    pf_vec = jnp.einsum("crk,ckn->crn", down_p, row_basis.astype(f32), precision=HIGH)
    down_q = jnp.einsum("rl,ckl->crk", qh_own, col_transfer.astype(f32), precision=HIGH)
    qf_vec = jnp.einsum("crk,ckn->crn", down_q, col_basis.astype(f32), precision=HIGH)
    half = 0.5 * mass[:, None, :]
    t_vec = half * p_dir.astype(f32) + pn_vec + pf_vec
    u_vec = half * q_dir.astype(f32) + qn_vec + qf_vec
    t_sq, u_sq = lax.psum(
        (jnp.sum(t_vec * t_vec, axis=(0, 2)), jnp.sum(u_vec * u_vec, axis=(0, 2))), ("clu", "sub")
    )
    rho = jnp.sqrt(t_sq + 1e-06)
    xi_norm = jnp.sqrt(u_sq + 1e-06)
    v_next = t_vec / rho[None, :, None]
    w_next = u_vec / xi_norm[None, :, None]
    delta = lax.psum(jnp.sum(v_next * w_next, axis=(0, 2)), ("clu", "sub"))
    return (v_next, w_next, delta)


def solution(mesh):
    return jax.shard_map(
        on_device,
        mesh=mesh,
        in_specs=(
            P("clu", None, "sub"),
            P("clu", None, "sub"),
            P("clu", "sub"),
            P("clu", None, None, "sub"),
            P("clu", None),
            P("clu"),
            P("clu", None, "sub"),
            P("clu", None, "sub"),
            P("clu", None, None),
            P("clu", None, None),
            P("clu", "sub", None, None),
            P("clu", "sub"),
        ),
        out_specs=(P("clu", None, "sub"), P("clu", None, "sub"), P()),
        check_vma=False,
    )
```

profile of v0, /device:TPU:1, one launch (start us, length us, event | category | flops | bytes accessed | tf_op | source)
XLA Modules:
  0.0 471.0 jit_solution(2710637620143292091)
XLA Ops:
  7.3 5.6 %collective-permute-start = (bf16[2,256,128]{2,1,0:T(8,128)(2,1)}, bf16[2,256,128]{2,1,0:T(8,128)(2,1)S(1)}, u32[]{:S(2)}, u32[]{:S(2)}) collective-permute-start(bf16[2,256,128]{2,1,0:T(8,128)(2,1)} %param.12), channel_id=1, source_target_pairs={{0,12},{4,16},{8,20},{12,24},{16,28},{20,32},{24,36},{28,40},{32,4... | collective-permute-start | bytes 393224 | tf_op jit(solution)/shard_map/ppermute | solution.py:16
  12.9 3.2 collective-permute-start.1
  16.1 2.2 collective-permute-start.2
  18.3 2.1 collective-permute-start.3
  20.4 1.3 collective-permute-start.4
  21.8 1.7 fusion.39
  23.5 1.8 fusion.40
  25.3 13.2 %all_gather.3 = bf16[2,256,512]{2,1,0:T(8,128)(2,1)S(1)} all-gather(bf16[2,256,128]{2,1,0:T(8,128)(2,1)} %param.13), channel_id=1, replica_groups=mesh['clu'=128,'sub'=4] {'sub'}, dimensions={2}, use_global_device_ids=true | all-gather | bytes 655360 | tf_op jit(solution)/shard_map/all_gather | solution.py:71
  43.8 10.5 %collective-permute-done.5 = bf16[2,256,128]{2,1,0:T(8,128)(2,1)S(1)} collective-permute-done((bf16[2,256,128]{2,1,0:T(8,128)(2,1)}, bf16[2,256,128]{2,1,0:T(8,128)(2,1)S(1)}, u32[]{:S(2)}, u32[]{:S(2)}) %collective-permute-start.5) | collective-permute-done | bytes 131104 | tf_op jit(solution)/shard_map/ppermute | solution.py:16
  54.3 2.2 gather_fusion
  56.5 25.5 %all-reduce.8.cloned.1.call-done = (f32[2,256,64]{1,2,0:T(8,128)}, f32[2,256,64]{2,1,0:T(8,128)}) async-done(((f32[2,256,64]{1,2,0:T(8,128)}, f32[2,256,64]{2,1,0:T(8,128)}), (f32[2,256,64]{1,2,0:T(8,128)}, f32[2,256,64]{2,1,0:T(8,128)})) %all-reduce.8.cloned.1.call-update) | async-done | bytes 262160 | tf_op jit(solution)/shard_map/psum | solution.py:39
  83.1 5.0 %collective-permute-start.6 = (f32[1,256,64]{1,2,0:T(8,128)S(1)}, f32[1,256,64]{1,2,0:T(8,128)S(1)}, u32[]{:S(2)}, u32[]{:S(2)}) collective-permute-start(f32[1,256,64]{1,2,0:T(8,128)S(1)} %convolution_bitcast_fusion.3), channel_id=1, source_target_pairs={{0,24},{4,28},{8,32},{12,36},{16,40},{20,44},{24,48},{28,52},{32,5... | collective-permute-start | bytes 196616 | tf_op jit(solution)/shard_map/ppermute | solution.py:16
  88.1 7.4 %collective-permute-start.7 = (f32[1,256,64]{1,2,0:T(8,128)S(1)}, f32[1,256,64]{1,2,0:T(8,128)S(1)}, u32[]{:S(2)}, u32[]{:S(2)}) collective-permute-start(f32[1,256,64]{1,2,0:T(8,128)S(1)} %convolution_bitcast_fusion.3), channel_id=1, source_target_pairs={{0,20},{4,24},{8,28},{12,32},{16,36},{20,40},{24,44},{28,48},{32,5... | collective-permute-start | bytes 196616 | tf_op jit(solution)/shard_map/ppermute | solution.py:16
  95.5 3.1 collective-permute-start.8
  98.6 1.3 collective-permute-start.9
  99.9 3.7 collective-permute-start.10
  107.1 4.9 %collective-permute-start.11 = (f32[1,256,64]{1,2,0:T(8,128)S(1)}, f32[1,256,64]{1,2,0:T(8,128)S(1)}, u32[]{:S(2)}, u32[]{:S(2)}) collective-permute-start(f32[1,256,64]{1,2,0:T(8,128)S(1)} %convolution_bitcast_fusion.3), channel_id=1, source_target_pairs={{0,4},{4,8},{8,12},{12,16},{16,20},{20,24},{24,28},{28,32},{32,36}... | collective-permute-start | bytes 196616 | tf_op jit(solution)/shard_map/ppermute | solution.py:16
  112.0 1.9 collective-permute-start.12
  114.0 1.3 collective-permute-start.13
  115.3 1.3 collective-permute-start.14
  120.6 10.1 %collective-permute-start.35 = (f32[1,256,64]{1,0,2:T(1,128)S(1)}, f32[1,256,64]{1,0,2:T(1,128)S(1)}, u32[]{:S(2)}, u32[]{:S(2)}) collective-permute-start(f32[1,256,64]{1,0,2:T(1,128)S(1)} %get-tuple-element.24), channel_id=1, source_target_pairs={{0,24},{4,28},{8,32},{12,36},{16,40},{20,44},{24,48},{28,52},{32,5... | collective-permute-start | bytes 196616 | tf_op jit(solution)/shard_map/ppermute | solution.py:16
  130.8 7.2 %collective-permute-start.34 = (f32[1,256,64]{1,0,2:T(1,128)S(1)}, f32[1,256,64]{1,0,2:T(1,128)S(1)}, u32[]{:S(2)}, u32[]{:S(2)}) collective-permute-start(f32[1,256,64]{1,0,2:T(1,128)S(1)} %get-tuple-element.25), channel_id=1, source_target_pairs={{0,20},{4,24},{8,28},{12,32},{16,36},{20,40},{24,44},{28,48},{32,5... | collective-permute-start | bytes 196616 | tf_op jit(solution)/shard_map/ppermute | solution.py:16
  138.0 6.6 %collective-permute-start.33 = (f32[1,256,64]{1,0,2:T(1,128)}, f32[1,256,64]{1,0,2:T(1,128)S(1)}, u32[]{:S(2)}, u32[]{:S(2)}) collective-permute-start(f32[1,256,64]{1,0,2:T(1,128)} %get-tuple-element.26), channel_id=1, source_target_pairs={{0,16},{4,20},{8,24},{12,28},{16,32},{20,36},{24,40},{28,44},{32,4... | collective-permute-start | bytes 196616 | tf_op jit(solution)/shard_map/ppermute | solution.py:16
  144.7 3.1 collective-permute-start.32
  147.8 3.4 collective-permute-start.31
  151.2 3.3 collective-permute-start.30
  154.6 1.9 collective-permute-start.29
  158.4 1.3 collective-permute-start.27
  162.3 1.3 collective-permute-start.24
  164.7 2.7 collective-permute-done.27
  167.4 4.0 collective-permute-done.26
  171.4 2.5 collective-permute-done.25
  173.9 1.9 collective-permute-done.24
  177.1 5.1 %fusion.4 = f32[2,256,512]{2,1,0:T(8,128)} fusion(bf16[2,16,512,128]{3,2,1,0:T(8,128)(2,1)} %param.15, bf16[2,16,256,128]{3,2,1,0:T(8,128)(2,1)} %bitcast.70, bf16[2,16]{1,0:T(2,128)(2,1)S(1)} %get-tuple-element.35), kind=kOutput, calls=%fused_computation.7 | convolution fusion | flops 1074790400 | bytes 7340096 | tf_op jit(solution)/shard_map/csmn,csrn->crm/dot_general | solution.py:69
  182.2 3.4 convolution_multiply_fusion
  185.7 3.9 fusion
  190.3 10.8 %collective-permute-start.23 = (f32[2,256,128]{2,1,0:T(8,128)S(1)}, f32[2,256,128]{2,1,0:T(8,128)S(1)}, u32[]{:S(2)}, u32[]{:S(2)}) collective-permute-start(f32[2,256,128]{2,1,0:T(8,128)S(1)} %copy.39), channel_id=1, source_target_pairs={{0,12},{4,16},{8,20},{12,24},{16,28},{20,32},{24,36},{28,40},{32,4... | collective-permute-start | bytes 786440 | tf_op jit(solution)/shard_map/ppermute | solution.py:16
  201.2 1.3 collective-permute-start.22
  202.5 3.1 collective-permute-start.21
  205.6 1.9 collective-permute-start.20
  207.6 1.3 collective-permute-start.19
  208.9 1.3 collective-permute-start.18
  210.2 25.3 %all-reduce.6.cloned.1.call-done = (f32[256,64]{1,0:T(8,128)}, f32[256,64]{0,1:T(8,128)}) async-done(((f32[256,64]{1,0:T(8,128)}, f32[256,64]{0,1:T(8,128)}), (f32[256,64]{1,0:T(8,128)}, f32[256,64]{0,1:T(8,128)})) %all-reduce.6.cloned.1.call-update) | async-done | bytes 131088 | tf_op jit(solution)/shard_map/psum | solution.py:104
  237.8 1.5 multiply_reduce_fusion.1
  239.3 29.2 %reduce-scatter.2.cloned.1.call-done = f32[2,256,128]{2,1,0:T(8,128)} async-done(((f32[2,256,512]{2,1,0:T(8,128)}), f32[2,256,128]{2,1,0:T(8,128)}) %reduce-scatter.2.cloned.1.call-update) | async-done | bytes 262160 | tf_op jit(solution)/shard_map/reduce_scatter | solution.py:70
  268.5 1.4 multiply_reduce_fusion.2
  269.9 98.3 %all-reduce = (f32[256]{0:T(256)S(1)}, f32[256]{0:T(256)S(1)}) all-reduce(f32[256]{0:T(256)S(1)} %get-tuple-element.37, f32[256]{0:T(256)S(1)} %get-tuple-element.12), channel_id=1, replica_groups=mesh['clu'=128,'sub'=4] {'clu','sub'}, use_global_device_ids=true, to_apply=%region_4.0 | all-reduce | flops 512 | bytes 4096 | tf_op jit(solution)/shard_map/psum | solution.py:112
  369.2 95.2 %psum.55 = f32[256]{0:T(256)} all-reduce(f32[256]{0:T(256)S(1)} %get-tuple-element.9), channel_id=1, replica_groups=mesh['clu'=128,'sub'=4] {'clu','sub'}, use_global_device_ids=true, to_apply=%region_10.0 | all-reduce | flops 256 | bytes 2048 | tf_op jit(solution)/shard_map/psum | solution.py:119
  (109 shorter events, 24.6 us)
Async XLA Ops:
  7.2 14.6 %copy-start = (bf16[2,64,128]{2,1,0:T(8,128)(2,1)S(1)}, bf16[2,64,128]{2,1,0:T(8,128)(2,1)}, u32[]{:S(2)}) copy-start(bf16[2,64,128]{2,1,0:T(8,128)(2,1)} %param.18) | copy-start | bytes 98308
  7.2 74.8 %copy-start.4 = (bf16[2,64,64]{2,1,0:T(8,128)(2,1)S(1)}, bf16[2,64,64]{2,1,0:T(8,128)(2,1)}, u32[]{:S(2)}) copy-start(bf16[2,64,64]{2,1,0:T(8,128)(2,1)} %param.20) | copy-start | bytes 49156
  7.2 96.5 %copy-start.5 = (bf16[2,64,64]{2,1,0:T(8,128)(2,1)S(1)}, bf16[2,64,64]{2,1,0:T(8,128)(2,1)}, u32[]{:S(2)}) copy-start(bf16[2,64,64]{2,1,0:T(8,128)(2,1)} %param.21) | copy-start | bytes 49156
  7.2 97.7 %copy-start.3 = (bf16[1,2,64,64]{3,2,1,0:T(8,128)(2,1)S(1)}, bf16[1,2,64,64]{3,2,1,0:T(8,128)(2,1)}, u32[]{:S(2)}) copy-start(bf16[1,2,64,64]{3,2,1,0:T(8,128)(2,1)} %param.22) | copy-start | bytes 49156
  7.2 74.8 %all-reduce.8.cloned.1.call-start = ((), (), s32[]{:S(2)}) async-start(), calls=%async_computation.3 | async-start | bytes 786432 | tf_op jit(solution)/shard_map/psum | solution.py:39
  7.3 34.1 %collective-permute-start = (bf16[2,256,128]{2,1,0:T(8,128)(2,1)}, bf16[2,256,128]{2,1,0:T(8,128)(2,1)S(1)}, u32[]{:S(2)}, u32[]{:S(2)}) collective-permute-start(bf16[2,256,128]{2,1,0:T(8,128)(2,1)} %param.12), channel_id=1, source_target_pairs={{0,12},{4,16},{8,20},{12,24},{16,28},{20,32},{24,36},{28,40},{32,4... | collective-permute-start | bytes 393224 | tf_op jit(solution)/shard_map/ppermute | solution.py:16
  12.9 29.8 %collective-permute-start.1 = (bf16[2,256,128]{2,1,0:T(8,128)(2,1)}, bf16[2,256,128]{2,1,0:T(8,128)(2,1)S(1)}, u32[]{:S(2)}, u32[]{:S(2)}) collective-permute-start(bf16[2,256,128]{2,1,0:T(8,128)(2,1)} %param.12), channel_id=1, source_target_pairs={{0,8},{4,12},{8,16},{12,20},{16,24},{20,28},{24,32},{28,36},{32,40... | collective-permute-start | bytes 393224 | tf_op jit(solution)/shard_map/ppermute | solution.py:16
  16.1 26.7 %collective-permute-start.2 = (bf16[2,256,128]{2,1,0:T(8,128)(2,1)}, bf16[2,256,128]{2,1,0:T(8,128)(2,1)S(1)}, u32[]{:S(2)}, u32[]{:S(2)}) collective-permute-start(bf16[2,256,128]{2,1,0:T(8,128)(2,1)} %param.12), channel_id=1, source_target_pairs={{0,4},{4,8},{8,12},{12,16},{16,20},{20,24},{24,28},{28,32},{32,36}... | collective-permute-start | bytes 393224 | tf_op jit(solution)/shard_map/ppermute | solution.py:16
  18.3 25.4 %collective-permute-start.3 = (bf16[2,256,128]{2,1,0:T(8,128)(2,1)}, bf16[2,256,128]{2,1,0:T(8,128)(2,1)S(1)}, u32[]{:S(2)}, u32[]{:S(2)}) collective-permute-start(bf16[2,256,128]{2,1,0:T(8,128)(2,1)} %param.12), channel_id=1, source_target_pairs={{4,0},{8,4},{12,8},{16,12},{20,16},{24,20},{28,24},{32,28},{36,32}... | collective-permute-start | bytes 393224 | tf_op jit(solution)/shard_map/ppermute | solution.py:16
  20.4 23.3 %collective-permute-start.4 = (bf16[2,256,128]{2,1,0:T(8,128)(2,1)}, bf16[2,256,128]{2,1,0:T(8,128)(2,1)S(1)}, u32[]{:S(2)}, u32[]{:S(2)}) collective-permute-start(bf16[2,256,128]{2,1,0:T(8,128)(2,1)} %param.12), channel_id=1, source_target_pairs={{8,0},{12,4},{16,8},{20,12},{24,16},{28,20},{32,24},{36,28},{40,32... | collective-permute-start | bytes 393224 | tf_op jit(solution)/shard_map/ppermute | solution.py:16
  25.3 210.3 %all-reduce.6.cloned.1.call-start = ((), (), s32[]{:S(2)}) async-start(), calls=%async_computation.2 | async-start | bytes 393216 | tf_op jit(solution)/shard_map/psum | solution.py:104
  41.4 12.9 %collective-permute-start.5 = (bf16[2,256,128]{2,1,0:T(8,128)(2,1)}, bf16[2,256,128]{2,1,0:T(8,128)(2,1)S(1)}, u32[]{:S(2)}, u32[]{:S(2)}) collective-permute-start(bf16[2,256,128]{2,1,0:T(8,128)(2,1)} %param.12), channel_id=1, source_target_pairs={{12,0},{16,4},{20,8},{24,12},{28,16},{32,20},{36,24},{40,28},{44,3... | collective-permute-start | bytes 393224 | tf_op jit(solution)/shard_map/ppermute | solution.py:16
  83.1 24.0 %collective-permute-start.6 = (f32[1,256,64]{1,2,0:T(8,128)S(1)}, f32[1,256,64]{1,2,0:T(8,128)S(1)}, u32[]{:S(2)}, u32[]{:S(2)}) collective-permute-start(f32[1,256,64]{1,2,0:T(8,128)S(1)} %convolution_bitcast_fusion.3), channel_id=1, source_target_pairs={{0,24},{4,28},{8,32},{12,36},{16,40},{20,44},{24,48},{28,52},{32,5... | collective-permute-start | bytes 196616 | tf_op jit(solution)/shard_map/ppermute | solution.py:16
  88.1 23.9 %collective-permute-start.7 = (f32[1,256,64]{1,2,0:T(8,128)S(1)}, f32[1,256,64]{1,2,0:T(8,128)S(1)}, u32[]{:S(2)}, u32[]{:S(2)}) collective-permute-start(f32[1,256,64]{1,2,0:T(8,128)S(1)} %convolution_bitcast_fusion.3), channel_id=1, source_target_pairs={{0,20},{4,24},{8,28},{12,32},{16,36},{20,40},{24,44},{28,48},{32,5... | collective-permute-start | bytes 196616 | tf_op jit(solution)/shard_map/ppermute | solution.py:16
  95.5 18.5 %collective-permute-start.8 = (f32[1,256,64]{1,2,0:T(8,128)S(1)}, f32[1,256,64]{1,2,0:T(8,128)S(1)}, u32[]{:S(2)}, u32[]{:S(2)}) collective-permute-start(f32[1,256,64]{1,2,0:T(8,128)S(1)} %convolution_bitcast_fusion.3), channel_id=1, source_target_pairs={{0,16},{4,20},{8,24},{12,28},{16,32},{20,36},{24,40},{28,44},{32,4... | collective-permute-start | bytes 196616 | tf_op jit(solution)/shard_map/ppermute | solution.py:16
  98.6 16.7 %collective-permute-start.9 = (f32[1,256,64]{1,2,0:T(8,128)S(1)}, f32[1,256,64]{1,2,0:T(8,128)S(1)}, u32[]{:S(2)}, u32[]{:S(2)}) collective-permute-start(f32[1,256,64]{1,2,0:T(8,128)S(1)} %convolution_bitcast_fusion.3), channel_id=1, source_target_pairs={{0,12},{4,16},{8,20},{12,24},{16,28},{20,32},{24,36},{28,40},{32,4... | collective-permute-start | bytes 196616 | tf_op jit(solution)/shard_map/ppermute | solution.py:16
  99.9 16.7 %collective-permute-start.10 = (f32[1,256,64]{1,2,0:T(8,128)S(1)}, f32[1,256,64]{1,2,0:T(8,128)S(1)}, u32[]{:S(2)}, u32[]{:S(2)}) collective-permute-start(f32[1,256,64]{1,2,0:T(8,128)S(1)} %convolution_bitcast_fusion.3), channel_id=1, source_target_pairs={{0,8},{4,12},{8,16},{12,20},{16,24},{20,28},{24,32},{28,36},{32,40... | collective-permute-start | bytes 196616 | tf_op jit(solution)/shard_map/ppermute | solution.py:16
  107.1 10.8 %collective-permute-start.11 = (f32[1,256,64]{1,2,0:T(8,128)S(1)}, f32[1,256,64]{1,2,0:T(8,128)S(1)}, u32[]{:S(2)}, u32[]{:S(2)}) collective-permute-start(f32[1,256,64]{1,2,0:T(8,128)S(1)} %convolution_bitcast_fusion.3), channel_id=1, source_target_pairs={{0,4},{4,8},{8,12},{12,16},{16,20},{20,24},{24,28},{28,32},{32,36}... | collective-permute-start | bytes 196616 | tf_op jit(solution)/shard_map/ppermute | solution.py:16
  112.0 7.3 %collective-permute-start.12 = (f32[1,256,64]{1,2,0:T(8,128)S(1)}, f32[1,256,64]{1,2,0:T(8,128)S(1)}, u32[]{:S(2)}, u32[]{:S(2)}) collective-permute-start(f32[1,256,64]{1,2,0:T(8,128)S(1)} %convolution_bitcast_fusion.3), channel_id=1, source_target_pairs={{4,0},{8,4},{12,8},{16,12},{20,16},{24,20},{28,24},{32,28},{36,32}... | collective-permute-start | bytes 196616 | tf_op jit(solution)/shard_map/ppermute | solution.py:16
  114.0 6.6 %collective-permute-start.13 = (f32[1,256,64]{1,2,0:T(8,128)S(1)}, f32[1,256,64]{1,2,0:T(8,128)S(1)}, u32[]{:S(2)}, u32[]{:S(2)}) collective-permute-start(f32[1,256,64]{1,2,0:T(8,128)S(1)} %convolution_bitcast_fusion.3), channel_id=1, source_target_pairs={{8,0},{12,4},{16,8},{20,12},{24,16},{28,20},{32,24},{36,28},{40,32... | collective-permute-start | bytes 196616 | tf_op jit(solution)/shard_map/ppermute | solution.py:16
  115.3 15.4 %collective-permute-start.14 = (f32[1,256,64]{1,2,0:T(8,128)S(1)}, f32[1,256,64]{1,2,0:T(8,128)S(1)}, u32[]{:S(2)}, u32[]{:S(2)}) collective-permute-start(f32[1,256,64]{1,2,0:T(8,128)S(1)} %convolution_bitcast_fusion.3), channel_id=1, source_target_pairs={{12,0},{16,4},{20,8},{24,12},{28,16},{32,20},{36,24},{40,28},{44,3... | collective-permute-start | bytes 196616 | tf_op jit(solution)/shard_map/ppermute | solution.py:16
  116.6 21.4 %collective-permute-start.15 = (f32[1,256,64]{1,2,0:T(8,128)S(1)}, f32[1,256,64]{1,2,0:T(8,128)S(1)}, u32[]{:S(2)}, u32[]{:S(2)}) collective-permute-start(f32[1,256,64]{1,2,0:T(8,128)S(1)} %convolution_bitcast_fusion.3), channel_id=1, source_target_pairs={{16,0},{20,4},{24,8},{28,12},{32,16},{36,20},{40,24},{44,28},{48,3... | collective-permute-start | bytes 196616 | tf_op jit(solution)/shard_map/ppermute | solution.py:16
  118.0 26.7 %collective-permute-start.16 = (f32[1,256,64]{1,2,0:T(8,128)S(1)}, f32[1,256,64]{1,2,0:T(8,128)S(1)}, u32[]{:S(2)}, u32[]{:S(2)}) collective-permute-start(f32[1,256,64]{1,2,0:T(8,128)S(1)} %convolution_bitcast_fusion.3), channel_id=1, source_target_pairs={{20,0},{24,4},{28,8},{32,12},{36,16},{40,20},{44,24},{48,28},{52,3... | collective-permute-start | bytes 196616 | tf_op jit(solution)/shard_map/ppermute | solution.py:16
  119.3 28.5 %collective-permute-start.17 = (f32[1,256,64]{1,2,0:T(8,128)S(1)}, f32[1,256,64]{1,2,0:T(8,128)S(1)}, u32[]{:S(2)}, u32[]{:S(2)}) collective-permute-start(f32[1,256,64]{1,2,0:T(8,128)S(1)} %convolution_bitcast_fusion.3), channel_id=1, source_target_pairs={{24,0},{28,4},{32,8},{36,12},{40,16},{44,20},{48,24},{52,28},{56,3... | collective-permute-start | bytes 196616 | tf_op jit(solution)/shard_map/ppermute | solution.py:16
  120.6 30.6 %collective-permute-start.35 = (f32[1,256,64]{1,0,2:T(1,128)S(1)}, f32[1,256,64]{1,0,2:T(1,128)S(1)}, u32[]{:S(2)}, u32[]{:S(2)}) collective-permute-start(f32[1,256,64]{1,0,2:T(1,128)S(1)} %get-tuple-element.24), channel_id=1, source_target_pairs={{0,24},{4,28},{8,32},{12,36},{16,40},{20,44},{24,48},{28,52},{32,5... | collective-permute-start | bytes 196616 | tf_op jit(solution)/shard_map/ppermute | solution.py:16
  130.8 23.8 %collective-permute-start.34 = (f32[1,256,64]{1,0,2:T(1,128)S(1)}, f32[1,256,64]{1,0,2:T(1,128)S(1)}, u32[]{:S(2)}, u32[]{:S(2)}) collective-permute-start(f32[1,256,64]{1,0,2:T(1,128)S(1)} %get-tuple-element.25), channel_id=1, source_target_pairs={{0,20},{4,24},{8,28},{12,32},{16,36},{20,40},{24,44},{28,48},{32,5... | collective-permute-start | bytes 196616 | tf_op jit(solution)/shard_map/ppermute | solution.py:16
  138.0 19.1 %collective-permute-start.33 = (f32[1,256,64]{1,0,2:T(1,128)}, f32[1,256,64]{1,0,2:T(1,128)S(1)}, u32[]{:S(2)}, u32[]{:S(2)}) collective-permute-start(f32[1,256,64]{1,0,2:T(1,128)} %get-tuple-element.26), channel_id=1, source_target_pairs={{0,16},{4,20},{8,24},{12,28},{16,32},{20,36},{24,40},{28,44},{32,4... | collective-permute-start | bytes 196616 | tf_op jit(solution)/shard_map/ppermute | solution.py:16
  144.7 13.7 %collective-permute-start.32 = (f32[1,256,64]{1,0,2:T(1,128)}, f32[1,256,64]{1,0,2:T(1,128)S(1)}, u32[]{:S(2)}, u32[]{:S(2)}) collective-permute-start(f32[1,256,64]{1,0,2:T(1,128)} %get-tuple-element.27), channel_id=1, source_target_pairs={{0,12},{4,16},{8,20},{12,24},{16,28},{20,32},{24,36},{28,40},{32,4... | collective-permute-start | bytes 196616 | tf_op jit(solution)/shard_map/ppermute | solution.py:16
  147.8 11.9 %collective-permute-start.31 = (f32[1,256,64]{1,0,2:T(1,128)}, f32[1,256,64]{1,0,2:T(1,128)S(1)}, u32[]{:S(2)}, u32[]{:S(2)}) collective-permute-start(f32[1,256,64]{1,0,2:T(1,128)} %get-tuple-element.28), channel_id=1, source_target_pairs={{0,8},{4,12},{8,16},{12,20},{16,24},{20,28},{24,32},{28,36},{32,40... | collective-permute-start | bytes 196616 | tf_op jit(solution)/shard_map/ppermute | solution.py:16
  151.2 9.8 %collective-permute-start.30 = (f32[1,256,64]{1,0,2:T(1,128)}, f32[1,256,64]{1,0,2:T(1,128)S(1)}, u32[]{:S(2)}, u32[]{:S(2)}) collective-permute-start(f32[1,256,64]{1,0,2:T(1,128)} %get-tuple-element.29), channel_id=1, source_target_pairs={{0,4},{4,8},{8,12},{12,16},{16,20},{20,24},{24,28},{28,32},{32,36}... | collective-permute-start | bytes 196616 | tf_op jit(solution)/shard_map/ppermute | solution.py:16
  154.6 7.8 %collective-permute-start.29 = (f32[1,256,64]{1,0,2:T(1,128)S(1)}, f32[1,256,64]{1,0,2:T(1,128)S(1)}, u32[]{:S(2)}, u32[]{:S(2)}) collective-permute-start(f32[1,256,64]{1,0,2:T(1,128)S(1)} %get-tuple-element.30), channel_id=1, source_target_pairs={{4,0},{8,4},{12,8},{16,12},{20,16},{24,20},{28,24},{32,28},{36,32}... | collective-permute-start | bytes 196616 | tf_op jit(solution)/shard_map/ppermute | solution.py:16
  157.1 7.6 %collective-permute-start.28 = (f32[1,256,64]{1,0,2:T(1,128)S(1)}, f32[1,256,64]{1,0,2:T(1,128)S(1)}, u32[]{:S(2)}, u32[]{:S(2)}) collective-permute-start(f32[1,256,64]{1,0,2:T(1,128)S(1)} %get-tuple-element.31), channel_id=1, source_target_pairs={{8,0},{12,4},{16,8},{20,12},{24,16},{28,20},{32,24},{36,28},{40,32... | collective-permute-start | bytes 196616 | tf_op jit(solution)/shard_map/ppermute | solution.py:16
  158.4 9.0 %collective-permute-start.27 = (f32[1,256,64]{1,0,2:T(1,128)S(1)}, f32[1,256,64]{1,0,2:T(1,128)S(1)}, u32[]{:S(2)}, u32[]{:S(2)}) collective-permute-start(f32[1,256,64]{1,0,2:T(1,128)S(1)} %get-tuple-element.32), channel_id=1, source_target_pairs={{12,0},{16,4},{20,8},{24,12},{28,16},{32,20},{36,24},{40,28},{44,3... | collective-permute-start | bytes 196616 | tf_op jit(solution)/shard_map/ppermute | solution.py:16
  159.7 11.7 %collective-permute-start.26 = (f32[1,256,64]{1,0,2:T(1,128)S(1)}, f32[1,256,64]{1,0,2:T(1,128)S(1)}, u32[]{:S(2)}, u32[]{:S(2)}) collective-permute-start(f32[1,256,64]{1,0,2:T(1,128)S(1)} %get-tuple-element.33), channel_id=1, source_target_pairs={{16,0},{20,4},{24,8},{28,12},{32,16},{36,20},{40,24},{44,28},{48,3... | collective-permute-start | bytes 196616 | tf_op jit(solution)/shard_map/ppermute | solution.py:16
  161.0 12.9 %collective-permute-start.25 = (f32[1,256,64]{1,0,2:T(1,128)S(1)}, f32[1,256,64]{1,0,2:T(1,128)S(1)}, u32[]{:S(2)}, u32[]{:S(2)}) collective-permute-start(f32[1,256,64]{1,0,2:T(1,128)S(1)} %get-tuple-element.34), channel_id=1, source_target_pairs={{20,0},{24,4},{28,8},{32,12},{36,16},{40,20},{44,24},{48,28},{52,3... | collective-permute-start | bytes 196616 | tf_op jit(solution)/shard_map/ppermute | solution.py:16
  162.3 13.5 %collective-permute-start.24 = (f32[1,256,64]{1,0,2:T(1,128)S(1)}, f32[1,256,64]{1,0,2:T(1,128)S(1)}, u32[]{:S(2)}, u32[]{:S(2)}) collective-permute-start(f32[1,256,64]{1,0,2:T(1,128)S(1)} %get-tuple-element.23), channel_id=1, source_target_pairs={{24,0},{28,4},{32,8},{36,12},{40,16},{44,20},{48,24},{52,28},{56,3... | collective-permute-start | bytes 196616 | tf_op jit(solution)/shard_map/ppermute | solution.py:16
  176.8 91.6 %reduce-scatter.2.cloned.1.call-start = ((), (), s32[]{:S(2)}) async-start(), calls=%async_computation.1 | async-start | bytes 1310720 | tf_op jit(solution)/shard_map/reduce_scatter | solution.py:70
  189.6 19.3 %copy-start.7 = (f32[2,128]{1,0:T(2,128)S(1)}, f32[2,128]{1,0:T(2,128)}, u32[]{:S(2)}) copy-start(f32[2,128]{1,0:T(2,128)} %param.14) | copy-start | bytes 3076
  189.6 48.2 %copy-start.2 = (bf16[2,256,128]{2,1,0:T(8,128)(2,1)S(1)}, bf16[2,256,128]{2,1,0:T(8,128)(2,1)}, u32[]{:S(2)}) copy-start(bf16[2,256,128]{2,1,0:T(8,128)(2,1)} %param.13) | copy-start | bytes 393220
  189.6 78.9 %copy-start.1 = (bf16[2,256,128]{2,1,0:T(8,128)(2,1)S(1)}, bf16[2,256,128]{2,1,0:T(8,128)(2,1)}, u32[]{:S(2)}) copy-start(bf16[2,256,128]{2,1,0:T(8,128)(2,1)} %param.12) | copy-start | bytes 393220
  189.6 78.9 %copy-start.6 = (bf16[2,64,128]{2,1,0:T(8,128)(2,1)S(1)}, bf16[2,64,128]{2,1,0:T(8,128)(2,1)}, u32[]{:S(2)}) copy-start(bf16[2,64,128]{2,1,0:T(8,128)(2,1)} %param.19) | copy-start | bytes 98308
  190.3 18.6 %collective-permute-start.23 = (f32[2,256,128]{2,1,0:T(8,128)S(1)}, f32[2,256,128]{2,1,0:T(8,128)S(1)}, u32[]{:S(2)}, u32[]{:S(2)}) collective-permute-start(f32[2,256,128]{2,1,0:T(8,128)S(1)} %copy.39), channel_id=1, source_target_pairs={{0,12},{4,16},{8,20},{12,24},{16,28},{20,32},{24,36},{28,40},{32,4... | collective-permute-start | bytes 786440 | tf_op jit(solution)/shard_map/ppermute | solution.py:16
  201.2 36.6 %collective-permute-start.22 = (f32[2,256,128]{2,1,0:T(8,128)S(1)}, f32[2,256,128]{2,1,0:T(8,128)S(1)}, u32[]{:S(2)}, u32[]{:S(2)}) collective-permute-start(f32[2,256,128]{2,1,0:T(8,128)S(1)} %copy.38), channel_id=1, source_target_pairs={{0,8},{4,12},{8,16},{12,20},{16,24},{20,28},{24,32},{28,36},{32,40... | collective-permute-start | bytes 786440 | tf_op jit(solution)/shard_map/ppermute | solution.py:16
  202.5 35.3 %collective-permute-start.21 = (f32[2,256,128]{2,1,0:T(8,128)S(1)}, f32[2,256,128]{2,1,0:T(8,128)S(1)}, u32[]{:S(2)}, u32[]{:S(2)}) collective-permute-start(f32[2,256,128]{2,1,0:T(8,128)S(1)} %copy.37), channel_id=1, source_target_pairs={{0,4},{4,8},{8,12},{12,16},{16,20},{20,24},{24,28},{28,32},{32,36}... | collective-permute-start | bytes 786440 | tf_op jit(solution)/shard_map/ppermute | solution.py:16
  205.6 32.2 %collective-permute-start.20 = (f32[2,256,128]{2,1,0:T(8,128)S(1)}, f32[2,256,128]{2,1,0:T(8,128)S(1)}, u32[]{:S(2)}, u32[]{:S(2)}) collective-permute-start(f32[2,256,128]{2,1,0:T(8,128)S(1)} %copy.36), channel_id=1, source_target_pairs={{4,0},{8,4},{12,8},{16,12},{20,16},{24,20},{28,24},{32,28},{36,32}... | collective-permute-start | bytes 786440 | tf_op jit(solution)/shard_map/ppermute | solution.py:16
  207.6 30.2 %collective-permute-start.19 = (f32[2,256,128]{2,1,0:T(8,128)S(1)}, f32[2,256,128]{2,1,0:T(8,128)S(1)}, u32[]{:S(2)}, u32[]{:S(2)}) collective-permute-start(f32[2,256,128]{2,1,0:T(8,128)S(1)} %copy.35), channel_id=1, source_target_pairs={{8,0},{12,4},{16,8},{20,12},{24,16},{28,20},{32,24},{36,28},{40,32... | collective-permute-start | bytes 786440 | tf_op jit(solution)/shard_map/ppermute | solution.py:16
  208.9 28.9 %collective-permute-start.18 = (f32[2,256,128]{2,1,0:T(8,128)S(1)}, f32[2,256,128]{2,1,0:T(8,128)}, u32[]{:S(2)}, u32[]{:S(2)}) collective-permute-start(f32[2,256,128]{2,1,0:T(8,128)S(1)} %copy.34), channel_id=1, source_target_pairs={{12,0},{16,4},{20,8},{24,12},{28,16},{32,20},{36,24},{40,28},{44,3... | collective-permute-start | bytes 786440 | tf_op jit(solution)/shard_map/ppermute | solution.py:16
Sparse Core Ops, SparseCore 0:
  25.4 56.5 all-reduce.7
  177.0 58.5 all-reduce.5
  238.4 30.0 reduce-scatter.1
where the time goes:
time: 472 us; the launch traced here: 471 us
  blocking collectives  207 us (44%)
  starting transfers between devices  112 us (24%)
  waiting for transfers between devices  102 us (22%)
  matrix products  25.5 us (5%)
  between operations  14.6 us (3%)
  local copies, waits for them, and re-layouts  6.69 us (1%)
    ppermute x36, starting transfers between devices, from_behind(): return lax.ppermute(block, axis, route)  111 us
    psum x1, blocking collectives, on_device(): lax.psum((jnp.sum(t_vec * t_vec, axis=(0, 2)), jnp.sum(u_vec * u_vec, axi...  98.3 us
    psum x1, blocking collectives, on_device(): delta = lax.psum(jnp.sum(v_next * w_next, axis=(0, 2)), ('clu', 'sub'))  95.2 us
    reduce_scatter x1, waiting for transfers between devices, on_device(): pn_vec = lax.psum_scatter(pn_part, 'sub', scatter_dimension=2, tiled=True)  29.2 us
    psum x1, waiting for transfers between devices, on_device(): pc_sum, qc_sum = lax.psum((pc_part, qc_part), 'sub')  25.5 us
    psum x1, waiting for transfers between devices, on_device(): ph_own, qh_own = lax.psum((ph_part, qh_part), 'sub')  25.3 us
    ppermute x36, waiting for transfers between devices, from_behind(): return lax.ppermute(block, axis, route)  21.7 us
    all_gather x1, blocking collectives, on_device(): q_rows = lax.all_gather(q_dir, 'sub', axis=2, tiled=True)  13.2 us
  transfers between devices with their start and end apart: 39, of which 8 were waited for; matrix products, arithmetic and copies ran while one was open for 7% of the time, Pallas kernels for 0%

commit v1 on v0

v1 whole, which is shorter than its diff:
```python
import functools

import jax
import jax.numpy as jnp
from jax import lax
from jax.experimental import pallas as pl
from jax.experimental.pallas import tpu as pltpu
from jax.sharding import PartitionSpec as P

NEAR = 3
FAR = 6
CORES = 2
CHIPS_Y = 8
MESH = pl.DeviceIdType.MESH
F32 = jnp.float32
BF16 = jnp.bfloat16
NEAR_SPAN = 2 * NEAR + 1
FAR_SPAN = 2 * FAR + 1


def mm(a, b):
    return lax.dot_general(a, b, (((1,), (0,)), ((), ())), preferred_element_type=F32)


def mm_nt(a, b):
    return lax.dot_general(a, b, (((1,), (1,)), ((), ())), preferred_element_type=F32)


def mm_tn(a, b):
    return lax.dot_general(a, b, (((0,), (0,)), ((), ())), preferred_element_type=F32)


def split(x):
    hi = x.astype(BF16)
    return hi, (x - hi.astype(F32)).astype(BF16)


def lane_half(shape):
    return lax.broadcasted_iota(jnp.int32, shape, 1) < shape[1] // 2


def kernel(
    sizes,
    table,
    p_ref,
    q_ref,
    mass_ref,
    col_ref,
    row_ref,
    colt_ref,
    rowt_ref,
    coup_ref,
    tiles_hbm,
    v_ref,
    w_ref,
    delta_ref,
    tiles,
    q_all,
    coup_all,
    p_win,
    up_part,
    up_recv,
    cw_hi,
    cw_lo,
    far_send,
    far_recv,
    chain,
    q_send,
    q_recv,
    pn_part,
    pn_recv,
    down_send,
    down_all,
    ar,
    tile_sem,
    q_ssem,
    q_rsem,
    c_ssem,
    c_rsem,
    p_ssem,
    p_rsem,
    up_ssem,
    up_rsem,
    far_ssem,
    far_rsem,
    qn_ssem,
    qn_rsem,
    pn_ssem,
    pn_rsem,
    down_ssem,
    down_rsem,
    ar_ssem,
    ar_rsem,
):
    n_clu, n_sub, n_y, slots = sizes
    n_z = n_clu // (n_y * CORES)
    clu = lax.axis_index("clu")
    sub = lax.axis_index("sub")
    core = lax.rem(clu, CORES)
    chip = clu // CORES
    y = lax.rem(chip, n_y)
    z = chip // n_y
    clusters, rhs, quarter = p_ref.shape
    block = rhs // n_sub

    def beside(offset):
        return (lax.rem(clu + (offset + n_clu), n_clu), sub)

    def peer(step):
        return lax.rem(sub + step, n_sub)

    groups = (
        (CORES * n_sub, sub * CORES + core, lambda i: (chip * CORES + lax.rem(i, CORES), i // CORES)),
        (n_y, y, lambda i: ((z * n_y + i) * CORES + core, sub)),
        (n_z, z, lambda i: ((i * n_y + y) * CORES + core, sub)),
    )

    def tile_copy(c):
        return pltpu.make_async_copy(tiles_hbm.at[c], tiles.at[c], tile_sem.at[c])

    for c in range(clusters):
        tile_copy(c).start()

    barrier = pltpu.get_barrier_semaphore()
    partners = 0
    for step in range(1, n_sub):
        pl.semaphore_signal(barrier, inc=1, device_id=(clu, peer(step)), device_id_type=MESH)
        partners += 1
    for offset in range(1, FAR + 1):
        for d in (-offset, offset):
            pl.semaphore_signal(barrier, inc=1, device_id=beside(d), device_id_type=MESH)
            partners += 1
    for size, mine, device in groups:
        for step in range(1, size):
            pl.semaphore_signal(barrier, inc=1, device_id=device(lax.rem(mine + step, size)), device_id_type=MESH)
            partners += 1

    q_all[sub] = q_ref[...]
    for j in range(coup_ref.shape[1]):
        own = coup_ref[0, j]
        coup_all[sub, j, :64] = jnp.concatenate([own, own], axis=1)
        coup_all[sub, j, 64:] = jnp.full((16, 128), table[78 + j].astype(F32), F32).astype(BF16)
    p_win[pl.ds(2 * NEAR, clusters)] = p_ref[...]
    p_win[2 * NEAR_SPAN] = jnp.zeros((rhs, quarter), BF16)
    chain[32] = jnp.zeros((rhs, quarter), F32)

    pl.semaphore_wait(barrier, partners)

    def to_peer(src, dst, ssem, rsem, step):
        return pltpu.make_async_remote_copy(
            src_ref=src, dst_ref=dst, send_sem=ssem, recv_sem=rsem, device_id=(clu, peer(step)), device_id_type=MESH
        )

    def to_side(src, dst, ssem, rsem, offset):
        return pltpu.make_async_remote_copy(
            src_ref=src, dst_ref=dst, send_sem=ssem, recv_sem=rsem, device_id=beside(offset), device_id_type=MESH
        )

    def q_copy(step):
        return to_peer(q_ref, q_all.at[sub], q_ssem.at[step - 1], q_rsem.at[step - 1], step)

    def c_copy(step):
        return to_peer(coup_all.at[sub], coup_all.at[sub], c_ssem.at[step - 1], c_rsem.at[step - 1], step)

    def up_copy(step):
        rows = pl.ds(pl.multiple_of(peer(step) * block, block), block)
        return to_peer(up_part.at[rows], up_recv.at[step - 1], up_ssem.at[step - 1], up_rsem.at[step - 1], step)

    def down_copy(step):
        return to_peer(down_send, down_all.at[sub], down_ssem.at[step - 1], down_rsem.at[step - 1], step)

    def pn_copy(step, c):
        return to_peer(
            pn_part.at[c, peer(step)],
            pn_recv.at[step - 1, c],
            pn_ssem.at[step - 1, c],
            pn_rsem.at[step - 1, c],
            step,
        )

    near_offsets = [d for k in range(NEAR, 0, -1) for d in (k, -k)]
    far_offsets = [d for k in range(FAR, 0, -1) for d in (k, -k)]

    def p_copy(i):
        d = near_offsets[i]
        there = (NEAR - d) * 2
        return to_side(p_ref, p_win.at[pl.ds(there, clusters)], p_ssem.at[i], p_rsem.at[i], d)

    def qn_copy(i):
        d = near_offsets[i]
        return to_side(q_send.at[i], q_recv.at[i], qn_ssem.at[i], qn_rsem.at[i], d)

    def far_copy(i):
        d = far_offsets[i]
        return to_side(far_send.at[i], far_recv.at[i], far_ssem.at[i], far_rsem.at[i], d)

    steps = range(1, n_sub)
    for step in steps:
        q_copy(step).start()
    for step in steps:
        c_copy(step).start()
    for i in range(len(near_offsets)):
        p_copy(i).start()

    up_hi, up_lo, down_hi, down_lo = [], [], [], []
    cols = [split(mm_tn(colt_ref[c], col_ref[c])) for c in range(clusters)]
    rows = [split(mm_tn(rowt_ref[c], row_ref[c])) for c in range(clusters)]
    none = jnp.zeros((cols[0][0].shape[0], clusters * quarter), BF16)
    col_hi, col_lo = (jnp.concatenate([x[k] for x in cols], axis=1) for k in range(2))
    row_hi, row_lo = (jnp.concatenate([x[k] for x in rows], axis=1) for k in range(2))

    def diagonal(a, b):
        return jnp.concatenate([jnp.concatenate([a, none], axis=1), jnp.concatenate([none, b], axis=1)], axis=0)

    both = jnp.concatenate([p_ref[0], p_ref[1], q_ref[0], q_ref[1]], axis=1)
    up_part[...] = mm_nt(both, diagonal(col_hi, row_hi)) + mm_nt(both, diagonal(col_lo, row_lo))
    for step in steps:
        up_copy(step).start()

    for step in steps:
        c_copy(step).wait()

    def gather_offset(w, carry):
        total = jnp.zeros((64, 128), F32)
        for s in range(n_sub):
            for j in range(coup_ref.shape[1]):
                here = coup_all[s, j, 64:65].astype(F32) == w.astype(F32)
                total = total + jnp.where(here, coup_all[s, j, :64].astype(F32), 0.0)
        hi, lo = split(total)
        cw_hi[w] = hi
        cw_lo[w] = lo
        return carry

    lax.fori_loop(0, FAR_SPAN, gather_offset, 0)

    for step in steps:
        up_copy(step).wait()
    up = up_part[pl.ds(pl.multiple_of(sub * block, block), block)]
    for step in steps:
        up = up + up_recv[step - 1]
    first = lane_half(up.shape)
    qg = up[:, 64:]
    qg_hi, qg_lo = split(qg)
    qg3 = jnp.concatenate([qg_hi, qg_lo, qg_hi], axis=1)

    def far_term(w):
        return mm(qg3, jnp.concatenate([cw_hi[w], cw_hi[w], cw_lo[w]], axis=0))

    for i, d in enumerate(far_offsets):
        far_send[i] = jnp.where(first, up, far_term(d + FAR))
        far_copy(i).start()
    own_far = jnp.where(first, up, far_term(FAR))

    for step in steps:
        q_copy(step).wait()
    for c in range(clusters):
        tile_copy(c).wait()
    for c in range(clusters):
        q_rows = jnp.concatenate([q_all[s, c] for s in range(n_sub)], axis=1)

        def back(k, carry, c=c, q_rows=q_rows):
            j = c * slots + 2 * k
            pair = jnp.concatenate([tiles[c, 2 * k], tiles[c, 2 * k + 1]], axis=1)
            out = mm(q_rows, pair)
            chain[j] = out[:, :quarter] + chain[table[j]]
            chain[j + 1] = out[:, quarter:] + chain[table[j + 1]]
            return carry

        lax.fori_loop(0, slots // 2, back, 0)
    for i, d in enumerate(near_offsets):
        for c in range(clusters):
            q_send[i, c] = chain[table[32 + 2 * (d + NEAR) + c]]
        qn_copy(i).start()

    for i in range(len(near_offsets)):
        p_copy(i).wait()
    for c in range(clusters):

        def front(k, carry, c=c):
            a = table[46 + c * slots + 2 * k]
            b = table[46 + c * slots + 2 * k + 1]
            source = jnp.concatenate([p_win[a], p_win[b]], axis=1)
            pair = jnp.concatenate([tiles[c, 2 * k], tiles[c, 2 * k + 1]], axis=1)
            out = mm_nt(source, pair)
            for s in range(n_sub):
                pn_part[c, s] += out[:, s * quarter : (s + 1) * quarter]
            return carry

        pn_part[c] = jnp.zeros_like(pn_part[c])
        lax.fori_loop(0, slots // 2, front, 0)
        for step in steps:
            pn_copy(step, c).start()

    def far_lhs(x):
        hi, lo = split(jnp.where(first, x, 0.0))
        return jnp.concatenate([hi, lo, hi], axis=1)

    def far_rhs(w):
        return jnp.concatenate([cw_hi[w], cw_hi[w], cw_lo[w]], axis=1)

    ph = mm_nt(far_lhs(own_far), far_rhs(FAR))
    total = own_far
    for i, d in enumerate(far_offsets):
        far_copy(i).wait()
        got = far_recv[i]
        ph = ph + mm_nt(far_lhs(got), far_rhs(FAR - d))
        total = total + got
    down_send[...] = jnp.where(first, jnp.concatenate([ph, ph], axis=1), total)
    for step in steps:
        down_copy(step).start()
    down_all[sub] = down_send[...]
    for step in steps:
        down_copy(step).wait()
    coeff = jnp.concatenate([down_all[s] for s in range(n_sub)], axis=0)
    coeff_hi, coeff_lo = split(coeff)
    coeff3 = jnp.concatenate([coeff_hi, coeff_lo, coeff_hi], axis=1)
    far_hi, far_lo = diagonal(row_hi, col_hi), diagonal(row_lo, col_lo)
    far_field = mm(coeff3, jnp.concatenate([far_hi, far_hi, far_lo], axis=0))

    for c in range(clusters):
        half = 0.5 * mass_ref[c : c + 1]
        v_ref[c] = half * p_ref[c].astype(F32) + far_field[:, c * quarter : (c + 1) * quarter]
        w_ref[c] = half * q_ref[c].astype(F32) + far_field[:, (clusters + c) * quarter : (clusters + c + 1) * quarter]

    for i in range(len(near_offsets)):
        qn_copy(i).wait()
    for c in range(clusters):
        u = w_ref[c] + chain[table[32 + 2 * NEAR + c]]
        for i in range(len(near_offsets)):
            u = u + q_recv[i, c]
        w_ref[c] = u
    for c in range(clusters):
        for step in steps:
            pn_copy(step, c).wait()
        t = v_ref[c] + pn_part[c, sub]
        for step in steps:
            t = t + pn_recv[step - 1, c]
        v_ref[c] = t

    def by_rhs(x):
        return jnp.sum(x.T, axis=0, keepdims=True)

    tt = by_rhs(v_ref[0] * v_ref[0] + v_ref[1] * v_ref[1])
    uu = by_rhs(w_ref[0] * w_ref[0] + w_ref[1] * w_ref[1])
    tu = by_rhs(v_ref[0] * w_ref[0] + v_ref[1] * w_ref[1])
    sums = jnp.concatenate([tt, uu, tu, jnp.zeros((5, rhs), F32)], axis=0)
    for g, (size, mine, device) in enumerate(groups):
        ar[g, mine] = sums

        def ar_copy(step, g=g, size=size, mine=mine, device=device):
            return pltpu.make_async_remote_copy(
                src_ref=ar.at[g, mine],
                dst_ref=ar.at[g, mine],
                send_sem=ar_ssem.at[g, step - 1],
                recv_sem=ar_rsem.at[g, step - 1],
                device_id=device(lax.rem(mine + step, size)),
                device_id_type=MESH,
            )

        for step in range(1, size):
            ar_copy(step).start()
        for step in range(1, size):
            ar_copy(step).wait()
        sums = ar[g, 0]
        for i in range(1, size):
            sums = sums + ar[g, i]

    rho = 1.0 / jnp.sqrt(sums[0:1] + 1e-06)
    xi = 1.0 / jnp.sqrt(sums[1:2] + 1e-06)
    delta_ref[...] = sums[2:3] * (rho * xi)
    rho_rows = jnp.broadcast_to(rho, (quarter, rhs)).T
    xi_rows = jnp.broadcast_to(xi, (quarter, rhs)).T
    for c in range(clusters):
        v_ref[c] = v_ref[c] * rho_rows
        w_ref[c] = w_ref[c] * xi_rows


def on_device(n_y, p_dir, q_dir, mass, tiles, near_ids, near_count, col, row, colt, rowt, coup, far_ids):
    clusters, rhs, quarter = p_dir.shape
    slots = tiles.shape[1]
    rank = col.shape[1]
    n_clu, n_sub = lax.axis_size("clu"), lax.axis_size("sub")
    block = rhs // n_sub
    here = lax.axis_index("clu")
    live = jnp.arange(slots, dtype=jnp.int32)[None, :] < near_count[:, None]
    local = near_ids - (here - NEAR) * clusters
    key = jnp.where(live, local, -1).reshape(-1)
    n_keys = clusters * slots
    wanted = jnp.concatenate([key, jnp.arange(clusters * NEAR_SPAN, dtype=jnp.int32)])
    limit = jnp.minimum(jnp.arange(wanted.shape[0], dtype=jnp.int32), n_keys)
    place = jnp.arange(n_keys, dtype=jnp.int32)
    same = (key[None, :] == wanted[:, None]) & (place[None, :] < limit[:, None])
    before = jnp.max(jnp.where(same, place[None, :], -1), axis=1)
    before = jnp.where(before < 0, n_keys, before)
    window = jnp.where(key < 0, clusters * NEAR_SPAN, key)
    table = jnp.concatenate([before, window, far_ids[0] - here + FAR])

    n_near, n_far = 2 * NEAR, 2 * FAR
    peers = n_sub - 1
    most = max(CORES * n_sub, n_y, n_clu // (n_y * CORES))
    vmem = pl.BlockSpec(memory_space=pltpu.VMEM)
    dma = pltpu.SemaphoreType.DMA
    v, w, delta = pl.pallas_call(
        functools.partial(kernel, (n_clu, n_sub, n_y, slots)),
        out_shape=(
            jax.ShapeDtypeStruct(p_dir.shape, F32),
            jax.ShapeDtypeStruct(p_dir.shape, F32),
            jax.ShapeDtypeStruct((1, rhs), F32),
        ),
        in_specs=[pl.BlockSpec(memory_space=pltpu.SMEM)] + [vmem] * 8 + [pl.BlockSpec(memory_space=pl.ANY)],
        out_specs=(vmem, vmem, vmem),
        scratch_shapes=[
            pltpu.VMEM(tiles.shape, BF16),
            pltpu.VMEM((n_sub, clusters, rhs, quarter), BF16),
            pltpu.VMEM((n_sub, coup.shape[1], rank + 16, 2 * rank), BF16),
            pltpu.VMEM((clusters * NEAR_SPAN + 1, rhs, quarter), BF16),
            pltpu.VMEM((rhs, 2 * rank), F32),
            pltpu.VMEM((peers, block, 2 * rank), F32),
            pltpu.VMEM((FAR_SPAN, rank, 2 * rank), BF16),
            pltpu.VMEM((FAR_SPAN, rank, 2 * rank), BF16),
            pltpu.VMEM((n_far, block, 2 * rank), F32),
            pltpu.VMEM((n_far, block, 2 * rank), F32),
            pltpu.VMEM((n_keys + 1, rhs, quarter), F32),
            pltpu.VMEM((n_near, clusters, rhs, quarter), F32),
            pltpu.VMEM((n_near, clusters, rhs, quarter), F32),
            pltpu.VMEM((clusters, n_sub, rhs, quarter), F32),
            pltpu.VMEM((peers, clusters, rhs, quarter), F32),
            pltpu.VMEM((block, 2 * rank), F32),
            pltpu.VMEM((n_sub, block, 2 * rank), F32),
            pltpu.VMEM((3, most, 8, rhs), F32),
            dma((clusters,)),
            dma((peers,)),
            dma((peers,)),
            dma((peers,)),
            dma((peers,)),
            dma((n_near,)),
            dma((n_near,)),
            dma((peers,)),
            dma((peers,)),
            dma((n_far,)),
            dma((n_far,)),
            dma((n_near,)),
            dma((n_near,)),
            dma((peers, clusters)),
            dma((peers, clusters)),
            dma((peers,)),
            dma((peers,)),
            dma((3, most)),
            dma((3, most)),
        ],
        compiler_params=pltpu.CompilerParams(
            collective_id=0, has_side_effects=True, vmem_limit_bytes=48 * 1024 * 1024
        ),
    )(table, p_dir, q_dir, mass, col, row, colt, rowt, coup, tiles)
    return v, w, delta.reshape(rhs)


def build(mesh, n_y):
    return jax.shard_map(
        functools.partial(on_device, n_y),
        mesh=mesh,
        in_specs=(
            P("clu", None, "sub"),
            P("clu", None, "sub"),
            P("clu", "sub"),
            P("clu", None, None, "sub"),
            P("clu", None),
            P("clu"),
            P("clu", None, "sub"),
            P("clu", None, "sub"),
            P("clu", None, None),
            P("clu", None, None),
            P("clu", "sub", None, None),
            P("clu", "sub"),
        ),
        out_specs=(P("clu", None, "sub"), P("clu", None, "sub"), P()),
        check_vma=False,
    )


def solution(mesh):
    return build(mesh, CHIPS_Y)
```

time: 472 us -> 78.9 us (0.17)
  blocking collectives: 207 us -> 0 us
  starting transfers between devices: 112 us -> 0 us
  waiting for transfers between devices: 102 us -> 0 us
  Pallas kernels: 0 us -> 65.4 us
  matrix products: 25.5 us -> 0 us
  between operations: 14.6 us -> 0.66 us
    psum x2 -> x0, blocking collectives: 194 us -> none  [the longest x1 98.3 us: on_device(): lax.psum((jnp.sum(t_vec * t_vec, axis=(0, 2)), jnp.sum(u_vec * u_vec, axi...]
    ppermute x36 -> x0, starting transfers between devices: 111 us -> none  [from_behind(): return lax.ppermute(block, axis, route)]
    pallas_call x0 -> x1, Pallas kernels: none -> 65.4 us  [on_device(): pl.pallas_call(functools.partial(kernel, (n_clu, n_sub, n_y, slots)), out...]
    psum x2 -> x0, waiting for transfers between devices: 50.8 us -> none  [the longest x1 25.5 us: on_device(): pc_sum, qc_sum = lax.psum((pc_part, qc_part), 'sub')]
    reduce_scatter x1 -> x0, waiting for transfers between devices: 29.2 us -> none  [on_device(): pn_vec = lax.psum_scatter(pn_part, 'sub', scatter_dimension=2, tiled=True)]
    dot_general x14 -> x0, matrix products: 25.5 us -> none  [the longest x1 5.11 us: on_device(): jnp.einsum('csmn,csrn->crm', nearby_tile_blocks, chosen, preferred_elemen...]
    ppermute x36 -> x0, waiting for transfers between devices: 21.7 us -> none  [from_behind(): return lax.ppermute(block, axis, route)]
    all_gather x1 -> x0, blocking collectives: 13.2 us -> none  [on_device(): q_rows = lax.all_gather(q_dir, 'sub', axis=2, tiled=True)]
  transfers between devices with their start and end apart: 39 -> 0, of which waited for: 8 -> 0; matrix products, arithmetic and copies ran while one was open for 7% -> 0% of each run, Pallas kernels for 0% -> 0%
where the time goes in v1:
time: 78.9 us; the launch traced here: 78.3 us
  Pallas kernels  65.4 us (83%)
  local copies, waits for them, and re-layouts  10.5 us (13%)
  other arithmetic  1.67 us (2%)
    pallas_call x1, Pallas kernels, on_device(): pl.pallas_call(functools.partial(kernel, (n_clu, n_sub, n_y, slots)), out...  65.4 us
    unnamed x21, local copies, waits for them, and re-layouts  10.4 us

profile of v1, /device:TPU:1, one launch (start us, length us, event | category | flops | bytes accessed | tf_op | source)
XLA Modules:
  0.0 78.3 jit_solution(7635972157668107003)
XLA Ops:
  0.6 0.7 add_bitcast_fusion
  1.3 0.8 compare_select_fusion.2
  2.0 0.1 eq.15
  2.1 0.1 pad_add_fusion
  2.2 0.1 select_reduce_fusion
  2.3 0.1 pad_add_fusion.1.table
  2.4 0.0 copy-start
  2.4 2.2 %copy-done = bf16[2,16,512,128]{3,2,1,0:T(8,128)(2,1)S(1)} copy-done((bf16[2,16,512,128]{3,2,1,0:T(8,128)(2,1)S(1)}, bf16[2,16,512,128]{3,2,1,0:T(8,128)(2,1)}, u32[]{:S(2)}) %copy-start) | copy-done | bytes 4194328
  4.6 0.0 copy-start.1
  4.6 0.9 %copy-done.1 = bf16[2,256,128]{2,1,0:T(8,128)(2,1)S(1)} copy-done((bf16[2,256,128]{2,1,0:T(8,128)(2,1)S(1)}, bf16[2,256,128]{2,1,0:T(8,128)(2,1)}, u32[]{:S(2)}) %copy-start.1) | copy-done | bytes 131096
  5.5 0.0 copy-start.2
  5.5 0.9 %copy-done.2 = bf16[2,256,128]{2,1,0:T(8,128)(2,1)S(1)} copy-done((bf16[2,256,128]{2,1,0:T(8,128)(2,1)S(1)}, bf16[2,256,128]{2,1,0:T(8,128)(2,1)}, u32[]{:S(2)}) %copy-start.2) | copy-done | bytes 131096
  6.4 0.0 copy-start.3
  6.4 0.8 copy-done.3
  7.2 0.0 copy-start.4
  7.2 0.8 copy-done.4
  7.9 0.0 copy-start.5
  7.9 0.8 copy-done.5
  8.7 0.0 copy-start.6
  8.7 0.8 copy-done.6
  9.4 0.0 copy-start.7
  9.4 0.8 copy-done.7
  10.2 0.0 copy-start.8
  10.2 0.7 copy-done.8
  10.9 65.4 %shard_map.139 = (f32[2,256,128]{2,1,0:T(8,128)S(1)}, f32[2,256,128]{2,1,0:T(8,128)S(1)}, f32[1,256]{1,0:T(1,128)S(1)}) custom-call(s32[80]{0:T(128)S(1)} %pad_add_fusion.1.table, bf16[2,256,128]{2,1,0:T(8,128)(2,1)S(1)} %copy-done.1, bf16[2,256,128]{2,1,0:T(8,128)(2,1)S(1)} %copy-done.2, f32[2,128]{1,0:T(2,128)S(1)} %copy-done.8, ...), custom_call_target="tpu_custom_call" | custom-call | tf_op jit(solution)/shard_map/pallas_call | solution.py:403
  76.3 0.7 copy.18
  77.0 0.7 copy.19
  77.7 0.6 copy.20
  (3 shorter events, 0.0 us)
Async XLA Ops:
  2.4 2.2 %copy-start = (bf16[2,16,512,128]{3,2,1,0:T(8,128)(2,1)S(1)}, bf16[2,16,512,128]{3,2,1,0:T(8,128)(2,1)}, u32[]{:S(2)}) copy-start(bf16[2,16,512,128]{3,2,1,0:T(8,128)(2,1)} %tiles_hbm.1) | copy-start | bytes 12582916
  4.6 0.9 %copy-start.1 = (bf16[2,256,128]{2,1,0:T(8,128)(2,1)S(1)}, bf16[2,256,128]{2,1,0:T(8,128)(2,1)}, u32[]{:S(2)}) copy-start(bf16[2,256,128]{2,1,0:T(8,128)(2,1)} %p_ref.1) | copy-start | bytes 393220
  5.5 0.9 %copy-start.2 = (bf16[2,256,128]{2,1,0:T(8,128)(2,1)S(1)}, bf16[2,256,128]{2,1,0:T(8,128)(2,1)}, u32[]{:S(2)}) copy-start(bf16[2,256,128]{2,1,0:T(8,128)(2,1)} %q_ref.1) | copy-start | bytes 393220
  6.4 0.8 copy-start.3
  7.2 0.8 copy-start.4
  7.9 0.8 copy-start.5
  8.7 0.8 copy-start.6
  9.4 0.8 copy-start.7
  10.2 0.7 copy-start.8

commit v2 on v1

v2 whole, which is shorter than its diff:
```python
import functools

import jax
import jax.numpy as jnp
from jax import lax
from jax.experimental import pallas as pl
from jax.experimental.pallas import tpu as pltpu
from jax.sharding import PartitionSpec as P

CORES = 2
CHIPS_Y = 8
NEAR_CHIPS = 2
FAR_CHIPS = 3
VMEM_BYTES = 64 * 1024 * 1024 - 64 * 1024
MESH = pl.DeviceIdType.MESH
F32 = jnp.float32
BF16 = jnp.bfloat16
NEAR_SPAN = CORES * (2 * NEAR_CHIPS + 1)
FAR_SPAN = CORES * (2 * FAR_CHIPS + 1)


def mm(a, b):
    return lax.dot_general(a, b, (((1,), (0,)), ((), ())), preferred_element_type=F32)


def mm_nt(a, b):
    return lax.dot_general(a, b, (((1,), (1,)), ((), ())), preferred_element_type=F32)


def mm_tn(a, b):
    return lax.dot_general(a, b, (((0,), (0,)), ((), ())), preferred_element_type=F32)


def split(x):
    hi = x.astype(BF16)
    return hi, (x - hi.astype(F32)).astype(BF16)


def lane_half(shape):
    return lax.broadcasted_iota(jnp.int32, shape, 1) < shape[1] // 2


def kernel(
    sizes,
    ids_ref,
    count_ref,
    far_ref,
    p_hbm,
    q_hbm,
    mass_hbm,
    col_hbm,
    row_hbm,
    colt_hbm,
    rowt_hbm,
    coup_hbm,
    tiles_hbm,
    t_hbm,
    u_hbm,
    scale_ref,
    table,
    t_ref,
    u_ref,
    mass_ref,
    col_ref,
    row_ref,
    colt_ref,
    rowt_ref,
    coup_ref,
    tiles,
    q_all,
    coup_all,
    p_win,
    up_part,
    up_recv,
    cw_hi,
    cw_lo,
    fx_send,
    fx_recv,
    far_send,
    far_recv,
    far_other,
    chain,
    ex_send,
    ex_recv,
    q_send,
    q_recv,
    pn_part,
    pn_recv,
    down_send,
    down_all,
    ar,
    out_sem,
    load_sem,
    tile_sem,
    q_ssem,
    q_rsem,
    c_ssem,
    c_rsem,
    p_ssem,
    p_rsem,
    up_ssem,
    up_rsem,
    fx_sem,
    far_ssem,
    far_rsem,
    ff_sem,
    ex_sem,
    qn_ssem,
    qn_rsem,
    pn_ssem,
    pn_rsem,
    down_ssem,
    down_rsem,
    ar_ssem,
    ar_rsem,
):
    n_clu, n_sub, n_y = sizes
    n_chips = n_clu // CORES
    n_z = n_chips // n_y
    clu = lax.axis_index("clu")
    sub = lax.axis_index("sub")
    core = lax.rem(clu, CORES)
    other = 1 - core
    chip = clu // CORES
    y = lax.rem(chip, n_y)
    z = chip // n_y
    toward = 2 * core - 1
    _, clusters, rhs, quarter = q_all.shape
    slots = tiles.shape[1]
    block = rhs // n_sub

    def on_chip(offset, which):
        return (lax.rem(chip + (offset + n_chips), n_chips) * CORES + which, sub)

    def peer(step):
        return lax.rem(sub + step, n_sub)

    sibling = (chip * CORES + other, sub)

    groups = (
        (CORES * n_sub, sub * CORES + core, lambda i: (chip * CORES + lax.rem(i, CORES), i // CORES)),
        (n_y, y, lambda i: ((z * n_y + i) * CORES + core, sub)),
        (n_z, z, lambda i: ((i * n_y + y) * CORES + core, sub)),
    )

    def near_parent(offset, which):
        return 2 * (NEAR_CHIPS + offset) + which

    def far_parent(offset, which):
        return 2 * (FAR_CHIPS + offset) + which

    def window(parent):
        return p_win.at[pl.ds(parent * clusters, clusters)]

    mine = near_parent(0, core)
    p_ref = window(mine)
    loads = [
        pltpu.make_async_copy(src, dst, load_sem.at[i])
        for i, (src, dst) in enumerate(
            (
                (p_hbm, p_ref),
                (q_hbm, q_all.at[sub]),
                (col_hbm, col_ref),
                (row_hbm, row_ref),
                (colt_hbm, colt_ref),
                (rowt_hbm, rowt_ref),
                (coup_hbm, coup_ref),
                (mass_hbm, mass_ref),
            )
        )
    ]

    def tile_copy(c):
        return pltpu.make_async_copy(tiles_hbm.at[c], tiles.at[c], tile_sem.at[c])

    barrier = pltpu.get_barrier_semaphore()
    partners = [device(lax.rem(place + step, size)) for size, place, device in groups for step in range(1, size)]
    partners += [on_chip(d, core) for k in range(1, FAR_CHIPS + 1) for d in (-k, k)]
    partners += [on_chip(2 * toward, other)]
    for partner in partners:
        pl.semaphore_signal(barrier, inc=1, device_id=partner, device_id_type=MESH)

    for load in loads:
        load.start()
    for c in range(clusters):
        tile_copy(c).start()

    n_keys = clusters * slots
    empty = p_win.shape[0] - 1
    at_last = n_keys
    at_block = n_keys + empty
    base = (chip - NEAR_CHIPS) * (CORES * clusters)
    for c in range(clusters):
        for s in range(slots):
            table[at_block + c * slots + s] = jnp.where(s < count_ref[c], ids_ref[c, s] - base, empty)

    def find(j, carry):
        wanted = table[at_block + j]
        found = jnp.int32(n_keys)
        for i in range(n_keys):
            found = jnp.where((table[at_block + i] == wanted) & (i < j), i, found)
        table[j] = found
        return carry

    def find_last(w, carry):
        found = jnp.int32(n_keys)
        for i in range(n_keys):
            found = jnp.where(table[at_block + i] == w, i, found)
        table[at_last + w] = found
        return carry

    p_win[empty] = jnp.zeros((rhs, quarter), BF16)
    chain[n_keys] = jnp.zeros((rhs, quarter), F32)
    for load in loads:
        load.wait()

    for j in range(coup_ref.shape[1]):
        coup_all[sub, j, :64] = coup_ref[0, j]
        far_place = far_ref[0, j] - (chip - FAR_CHIPS) * CORES
        coup_all[sub, j, 64:] = jnp.full((16, 64), far_place.astype(F32), F32).astype(BF16)

    cols = [split(mm_tn(colt_ref[c], col_ref[c])) for c in range(clusters)]
    rows = [split(mm_tn(rowt_ref[c], row_ref[c])) for c in range(clusters)]
    none = jnp.zeros((cols[0][0].shape[0], clusters * quarter), BF16)
    col_hi, col_lo = (jnp.concatenate([x[k] for x in cols], axis=1) for k in range(2))
    row_hi, row_lo = (jnp.concatenate([x[k] for x in rows], axis=1) for k in range(2))

    def diagonal(a, b):
        return jnp.concatenate([jnp.concatenate([a, none], axis=1), jnp.concatenate([none, b], axis=1)], axis=0)

    both = jnp.concatenate([p_ref[0], p_ref[1], q_all[sub, 0], q_all[sub, 1]], axis=1)
    up_part[...] = mm_nt(both, diagonal(col_hi, row_hi)) + mm_nt(both, diagonal(col_lo, row_lo))

    pl.semaphore_wait(barrier, len(partners))

    def remote(src, dst, ssem, rsem, device):
        return pltpu.make_async_remote_copy(
            src_ref=src, dst_ref=dst, send_sem=ssem, recv_sem=rsem, device_id=device, device_id_type=MESH
        )

    def to_peer(src, dst, ssem, rsem, step):
        return remote(src, dst, ssem, rsem, (clu, peer(step)))

    def q_copy(step):
        return to_peer(q_all.at[sub], q_all.at[sub], q_ssem.at[step - 1], q_rsem.at[step - 1], step)

    def c_copy(step):
        return to_peer(coup_all.at[sub], coup_all.at[sub], c_ssem.at[step - 1], c_rsem.at[step - 1], step)

    def up_copy(step):
        rows = pl.ds(pl.multiple_of(peer(step) * block, block), block)
        return to_peer(up_part.at[rows], up_recv.at[step - 1], up_ssem.at[step - 1], up_rsem.at[step - 1], step)

    def down_copy(step):
        return to_peer(down_send, down_all.at[sub], down_ssem.at[step - 1], down_rsem.at[step - 1], step)

    def pn_copy(step, c):
        return to_peer(
            pn_part.at[c, peer(step)],
            pn_recv.at[step - 1, c],
            pn_ssem.at[step - 1, c],
            pn_rsem.at[step - 1, c],
            step,
        )

    sides = (1, -1)

    def p_copy(i):
        if i < 2:
            source, there, device = mine, near_parent(-sides[i], core), on_chip(sides[i], core)
        elif i == 2:
            source, there, device = mine, near_parent(-2 * toward, core), on_chip(2 * toward, other)
        elif i == 3:
            source, there, device = mine, mine, sibling
        else:
            source = there = near_parent(-sides[i - 4], core)
            device = sibling
        return remote(window(source), window(there), p_ssem.at[i], p_rsem.at[i], device)

    far_sides = tuple(d for k in range(FAR_CHIPS, 0, -1) for d in (k, -k))

    def fx_copy():
        return remote(fx_send, fx_recv, fx_sem.at[0], fx_sem.at[1], sibling)

    def far_copy(i):
        return remote(far_send.at[i], far_recv.at[i], far_ssem.at[i], far_rsem.at[i], on_chip(far_sides[i], core))

    def ff_copy():
        return remote(far_recv, far_other, ff_sem.at[0], ff_sem.at[1], sibling)

    def ex_copy(e):
        return remote(ex_send.at[e + 1], ex_recv.at[e + 1], ex_sem.at[0, e + 1], ex_sem.at[1, e + 1], sibling)

    def qn_copy(i):
        device = on_chip(sides[i], core) if i < 2 else on_chip(2 * toward, other)
        return remote(q_send.at[i], q_recv.at[i], qn_ssem.at[i], qn_rsem.at[i], device)

    steps = range(1, n_sub)
    for step in steps:
        up_copy(step).start()
    for i in range(4):
        p_copy(i).start()
    for step in steps:
        c_copy(step).start()
    for step in steps:
        q_copy(step).start()

    lax.fori_loop(0, n_keys, find, 0)
    lax.fori_loop(0, empty, find_last, 0)

    for step in steps:
        c_copy(step).wait()

    def gather_offset(w, carry):
        total = jnp.zeros((64, 64), F32)
        for s in range(n_sub):
            for j in range(coup_ref.shape[1]):
                here = coup_all[s, j, 64:65].astype(F32) == w.astype(F32)
                total = total + jnp.where(here, coup_all[s, j, :64].astype(F32), 0.0)
        hi, lo = split(jnp.concatenate([total, total], axis=1))
        cw_hi[w] = hi
        cw_lo[w] = lo
        return carry

    lax.fori_loop(0, FAR_SPAN, gather_offset, 0)

    for step in steps:
        up_copy(step).wait()
    up = up_part[pl.ds(pl.multiple_of(sub * block, block), block)]
    for step in steps:
        up = up + up_recv[step - 1]
    first = lane_half(up.shape)
    qg_hi, qg_lo = split(up[:, 64:])
    qg3 = jnp.concatenate([qg_hi, qg_lo, qg_hi], axis=1)

    def far_term(w):
        return mm(qg3, jnp.concatenate([cw_hi[w], cw_hi[w], cw_lo[w]], axis=0))

    for e in range(-FAR_CHIPS, FAR_CHIPS + 1):
        fx_send[e + FAR_CHIPS] = far_term(far_parent(e, other))
    fx_copy().start()
    far_own = [far_term(far_parent(e, core)) for e in range(-FAR_CHIPS, FAR_CHIPS + 1)]
    far_recv[2 * FAR_CHIPS] = up
    fx_copy().wait()

    def far_tile(e):
        return jnp.where(first, up, far_own[e + FAR_CHIPS] + fx_recv[e + FAR_CHIPS])

    for i, e in enumerate(far_sides):
        far_send[i] = far_tile(e)
        far_copy(i).start()
    own_tile = far_tile(0)

    for i in range(2):
        p_copy(i).wait()
        p_copy(4 + i).start()

    for step in steps:
        q_copy(step).wait()
    for c in range(clusters):
        tile_copy(c).wait()
    for c in range(clusters):
        q_rows = jnp.concatenate([q_all[s, c] for s in range(n_sub)], axis=1)

        def back(k, carry, c=c, q_rows=q_rows):
            j = c * slots + 2 * k
            pair = jnp.concatenate([tiles[c, 2 * k], tiles[c, 2 * k + 1]], axis=1)
            out = mm(q_rows, pair)
            chain[j] = out[:, :quarter] + chain[table[j]]
            chain[j + 1] = out[:, quarter:] + chain[table[j + 1]]
            return carry

        lax.fori_loop(0, slots // 2, back, 0, unroll=slots // 2)

    def back_to(parent, c):
        return chain[table[at_last + clusters * parent + c]]

    for e in (1, -1, 0):
        for c in range(clusters):
            ex_send[e + 1, c] = back_to(near_parent(e, other), c)
        ex_copy(e).start()
    for c in range(clusters):
        q_send[2, c] = back_to(near_parent(2 * toward, other), c)
    qn_copy(2).start()

    for i in range(2, 6):
        p_copy(i).wait()

    def near_products(c):
        def front(k, carry):
            a = table[at_block + c * slots + 2 * k]
            b = table[at_block + c * slots + 2 * k + 1]
            source = jnp.concatenate([p_win[a], p_win[b]], axis=1)
            pair = jnp.concatenate([tiles[c, 2 * k], tiles[c, 2 * k + 1]], axis=1)
            out = mm_nt(source, pair)
            for s in range(n_sub):
                pn_part[c, s] += out[:, s * quarter : (s + 1) * quarter]
            return carry

        pn_part[c] = jnp.zeros_like(pn_part[c])
        lax.fori_loop(0, slots // 2, front, 0, unroll=slots // 2)
        for step in steps:
            pn_copy(step, c).start()

    near_products(0)
    for i, e in enumerate(sides):
        ex_copy(e).wait()
        for c in range(clusters):
            q_send[i, c] = back_to(near_parent(e, core), c) + ex_recv[e + 1, c]
        qn_copy(i).start()
    for c in range(1, clusters):
        near_products(c)

    def far_lhs(x):
        hi, lo = split(jnp.where(first, x, 0.0))
        return jnp.concatenate([hi, lo, hi], axis=1)

    def far_rhs(w):
        return jnp.concatenate([cw_hi[w], cw_hi[w], cw_lo[w]], axis=1)

    for i in range(len(far_sides)):
        far_copy(i).wait()
    ff_copy().start()
    ph = mm_nt(far_lhs(own_tile), far_rhs(far_parent(0, core)))
    total = own_tile
    for i, e in enumerate(far_sides):
        got = far_recv[i]
        ph = ph + mm_nt(far_lhs(got), far_rhs(far_parent(-e, core)))
        total = total + got
    ff_copy().wait()
    for i, e in enumerate(far_sides + (0,)):
        ph = ph + mm_nt(far_lhs(far_other[i]), far_rhs(far_parent(-e, other)))

    down_send[...] = jnp.where(first, jnp.concatenate([ph, ph], axis=1), total)
    for step in steps:
        down_copy(step).start()
    down_all[sub] = down_send[...]
    for step in steps:
        down_copy(step).wait()
    coeff = jnp.concatenate([down_all[s] for s in range(n_sub)], axis=0)
    coeff_hi, coeff_lo = split(coeff)
    coeff3 = jnp.concatenate([coeff_hi, coeff_lo, coeff_hi], axis=1)
    far_hi, far_lo = diagonal(row_hi, col_hi), diagonal(row_lo, col_lo)
    far_field = mm(coeff3, jnp.concatenate([far_hi, far_hi, far_lo], axis=0))

    ex_copy(0).wait()
    for c in range(clusters):
        half = 0.5 * mass_ref[c : c + 1]
        t_ref[c] = half * p_ref[c].astype(F32) + far_field[:, c * quarter : (c + 1) * quarter] + pn_part[c, sub]
        u = half * q_all[sub, c].astype(F32) + far_field[:, (clusters + c) * quarter : (clusters + c + 1) * quarter]
        u_ref[c] = u + (back_to(mine, c) + ex_recv[1, c])

    for c in range(clusters):
        for step in steps:
            pn_copy(step, c).wait()
        t = t_ref[c]
        for step in steps:
            t = t + pn_recv[step - 1, c]
        t_ref[c] = t
    for i in range(3):
        qn_copy(i).wait()
    for c in range(clusters):
        u_ref[c] = u_ref[c] + (q_recv[0, c] + q_recv[1, c] + q_recv[2, c])

    outs = [
        pltpu.make_async_copy(src, dst, out_sem.at[i]) for i, (src, dst) in enumerate(((t_ref, t_hbm), (u_ref, u_hbm)))
    ]
    for out in outs:
        out.start()

    def by_rhs(x):
        return jnp.sum(x.T, axis=0, keepdims=True)

    tt = by_rhs(t_ref[0] * t_ref[0] + t_ref[1] * t_ref[1])
    uu = by_rhs(u_ref[0] * u_ref[0] + u_ref[1] * u_ref[1])
    tu = by_rhs(t_ref[0] * u_ref[0] + t_ref[1] * u_ref[1])
    sums = jnp.concatenate([tt, uu, tu, jnp.zeros((5, rhs), F32)], axis=0)
    for g, (size, place, device) in enumerate(groups):
        ar[g, place] = sums

        def ar_copy(step, g=g, size=size, place=place, device=device):
            return pltpu.make_async_remote_copy(
                src_ref=ar.at[g, place],
                dst_ref=ar.at[g, place],
                send_sem=ar_ssem.at[g, step - 1],
                recv_sem=ar_rsem.at[g, step - 1],
                device_id=device(lax.rem(place + step, size)),
                device_id_type=MESH,
            )

        for step in range(1, size):
            ar_copy(step).start()
        for step in range(1, size):
            ar_copy(step).wait()
        sums = ar[g, 0]
        for i in range(1, size):
            sums = sums + ar[g, i]

    rho = 1.0 / jnp.sqrt(sums[0:1] + 1e-06)
    xi = 1.0 / jnp.sqrt(sums[1:2] + 1e-06)
    delta = sums[2:3] * (rho * xi)
    scale_ref[...] = jnp.concatenate([rho, xi, delta, jnp.zeros((5, rhs), F32)], axis=0)
    for out in outs:
        out.wait()


def scale_kernel(scale_ref, t_ref, u_ref, v_ref, w_ref, delta_ref):
    rhs, quarter = t_ref.shape[1:]
    v_ref[0] = t_ref[0] * jnp.broadcast_to(scale_ref[0:1], (quarter, rhs)).T
    w_ref[0] = u_ref[0] * jnp.broadcast_to(scale_ref[1:2], (quarter, rhs)).T
    delta_ref[...] = scale_ref[2:3]


def on_device(n_y, p_dir, q_dir, mass, tiles, near_ids, near_count, col, row, colt, rowt, coup, far_ids):
    clusters, rhs, quarter = p_dir.shape
    slots = tiles.shape[1]
    rank = col.shape[1]
    n_clu, n_sub = lax.axis_size("clu"), lax.axis_size("sub")
    block = rhs // n_sub
    n_keys = clusters * slots
    peers = n_sub - 1
    sides = 2 * FAR_CHIPS
    most = max(CORES * n_sub, n_y, n_clu // (n_y * CORES))
    vmem = pl.BlockSpec(memory_space=pltpu.VMEM)
    smem = pl.BlockSpec(memory_space=pltpu.SMEM)
    hbm = pl.BlockSpec(memory_space=pltpu.HBM)
    dma = pltpu.SemaphoreType.DMA
    whole = (clusters, rhs, quarter)
    t, u, scale = pl.pallas_call(
        functools.partial(kernel, (n_clu, n_sub, n_y)),
        out_shape=(
            jax.ShapeDtypeStruct(whole, F32),
            jax.ShapeDtypeStruct(whole, F32),
            jax.ShapeDtypeStruct((8, rhs), F32),
        ),
        in_specs=[smem] * 3 + [hbm] * 9,
        out_specs=(hbm, hbm, vmem),
        scratch_shapes=[
            pltpu.SMEM((2 * n_keys + clusters * NEAR_SPAN,), jnp.int32),
            pltpu.VMEM(whole, F32),
            pltpu.VMEM(whole, F32),
            pltpu.VMEM(mass.shape, F32),
            pltpu.VMEM(col.shape, BF16),
            pltpu.VMEM(col.shape, BF16),
            pltpu.VMEM(colt.shape, BF16),
            pltpu.VMEM(colt.shape, BF16),
            pltpu.VMEM(coup.shape, BF16),
            pltpu.VMEM(tiles.shape, BF16),
            pltpu.VMEM((n_sub, *whole), BF16),
            pltpu.VMEM((n_sub, coup.shape[1], rank + 16, rank), BF16),
            pltpu.VMEM((clusters * NEAR_SPAN + 1, rhs, quarter), BF16),
            pltpu.VMEM((rhs, 2 * rank), F32),
            pltpu.VMEM((peers, block, 2 * rank), F32),
            pltpu.VMEM((FAR_SPAN, rank, 2 * rank), BF16),
            pltpu.VMEM((FAR_SPAN, rank, 2 * rank), BF16),
            pltpu.VMEM((sides + 1, block, 2 * rank), F32),
            pltpu.VMEM((sides + 1, block, 2 * rank), F32),
            pltpu.VMEM((sides, block, 2 * rank), F32),
            pltpu.VMEM((sides + 1, block, 2 * rank), F32),
            pltpu.VMEM((sides + 1, block, 2 * rank), F32),
            pltpu.VMEM((n_keys + 1, rhs, quarter), F32),
            pltpu.VMEM((3, *whole), F32),
            pltpu.VMEM((3, *whole), F32),
            pltpu.VMEM((3, *whole), F32),
            pltpu.VMEM((3, *whole), F32),
            pltpu.VMEM((clusters, n_sub, rhs, quarter), F32),
            pltpu.VMEM((peers, *whole), F32),
            pltpu.VMEM((block, 2 * rank), F32),
            pltpu.VMEM((n_sub, block, 2 * rank), F32),
            pltpu.VMEM((3, most, 8, rhs), F32),
            dma((2,)),
            dma((8,)),
            dma((clusters,)),
            dma((peers,)),
            dma((peers,)),
            dma((peers,)),
            dma((peers,)),
            dma((6,)),
            dma((6,)),
            dma((peers,)),
            dma((peers,)),
            dma((2,)),
            dma((sides,)),
            dma((sides,)),
            dma((2,)),
            dma((2, 3)),
            dma((3,)),
            dma((3,)),
            dma((peers, clusters)),
            dma((peers, clusters)),
            dma((peers,)),
            dma((peers,)),
            dma((3, most)),
            dma((3, most)),
        ],
        compiler_params=pltpu.CompilerParams(
            collective_id=0, has_side_effects=True, vmem_limit_bytes=VMEM_BYTES
        ),
    )(near_ids, near_count, far_ids, p_dir, q_dir, mass, col, row, colt, rowt, coup, tiles)
    one = pl.BlockSpec((1, rhs, quarter), lambda c: (c, 0, 0))
    v, w, delta = pl.pallas_call(
        scale_kernel,
        grid=(clusters,),
        out_shape=(
            jax.ShapeDtypeStruct(whole, F32),
            jax.ShapeDtypeStruct(whole, F32),
            jax.ShapeDtypeStruct((1, rhs), F32),
        ),
        in_specs=[pl.BlockSpec((8, rhs), lambda c: (0, 0)), one, one],
        out_specs=(one, one, pl.BlockSpec((1, rhs), lambda c: (0, 0))),
        compiler_params=pltpu.CompilerParams(vmem_limit_bytes=VMEM_BYTES),
    )(scale, t, u)
    return v, w, delta.reshape(rhs)


def build(mesh, n_y):
    return jax.shard_map(
        functools.partial(on_device, n_y),
        mesh=mesh,
        in_specs=(
            P("clu", None, "sub"),
            P("clu", None, "sub"),
            P("clu", "sub"),
            P("clu", None, None, "sub"),
            P("clu", None),
            P("clu"),
            P("clu", None, "sub"),
            P("clu", None, "sub"),
            P("clu", None, None),
            P("clu", None, None),
            P("clu", "sub", None, None),
            P("clu", "sub"),
        ),
        out_specs=(P("clu", None, "sub"), P("clu", None, "sub"), P()),
        check_vma=False,
    )


def solution(mesh):
    return build(mesh, CHIPS_Y)
```

time: 78.9 us -> 61.5 us (0.78)
  local copies, waits for them, and re-layouts: 10.5 us -> 0 us
  Pallas kernels: 65.4 us -> 60.7 us
  other arithmetic: 1.67 us -> 0 us
    unnamed x21 -> x0, local copies, waits for them, and re-layouts: 10.4 us -> none
    pallas_call x1 -> x2, Pallas kernels: 65.4 us -> 60.7 us  [the longest x1 58.7 us: on_device(): pl.pallas_call(functools.partial(kernel, (n_clu, n_sub, n_y)), out_shape=...]
where the time goes in v2:
time: 61.5 us; the launch traced here: 61.3 us
  Pallas kernels  60.7 us (99%)
  between operations  0.64 us (1%)
    pallas_call x1, Pallas kernels, on_device(): pl.pallas_call(functools.partial(kernel, (n_clu, n_sub, n_y)), out_shape=...  58.7 us
    pallas_call x1, Pallas kernels, on_device(): pl.pallas_call(scale_kernel, grid=(clusters,), out_shape=(jax.ShapeDtypeS...  1.95 us

profile of v2, /device:TPU:1, one launch (start us, length us, event | category | flops | bytes accessed | tf_op | source)
XLA Modules:
  0.0 61.3 jit_solution(2994223067357858662)
XLA Ops:
  0.6 58.7 %shard_map.139 = (f32[2,256,128]{2,1,0:T(8,128)}, f32[2,256,128]{2,1,0:T(8,128)}, f32[8,256]{1,0:T(8,128)}) custom-call(s32[2,16]{1,0:T(2,128)} %ids_ref.1, s32[2]{0:T(128)} %count_ref.1, s32[1,2]{1,0:T(1,128)} %far_ref.1, bf16[2,256,128]{2,1,0:T(8,128)(2,1)} %p_hbm.1, bf16[2,256,128]{2,1,0:T(8,128)(2,1)} %q_hbm.1, f32[2,128]{1,0:T(2,128)} %mass_hbm.1, ...), custom_call_target="tpu_custom_call" | custom-call | tf_op jit(solution)/shard_map/pallas_call | solution.py:529
  59.4 1.9 %shard_map.140 = (f32[2,256,128]{2,1,0:T(8,128)}, f32[2,256,128]{2,1,0:T(8,128)}, f32[1,256]{1,0:T(1,128)}) custom-call(f32[8,256]{1,0:T(8,128)} %get-tuple-element.9.scale_ref, f32[2,256,128]{2,1,0:T(8,128)} %get-tuple-element.10.t_ref, f32[2,256,128]{2,1,0:T(8,128)} %get-tuple-element.11.u_ref), custom_call_target="tpu_custom_call" | custom-call | tf_op jit(solution)/shard_map/pallas_call | solution.py:601

commit v3 on v2

--- a/solution.py
+++ b/solution.py
@@ -85,6 +85,7 @@
     q_send,
     q_recv,
     pn_part,
+    pn_mid,
     pn_recv,
     down_send,
     down_all,
@@ -107,6 +108,7 @@
     ex_sem,
     qn_ssem,
     qn_rsem,
+    mid_sem,
     pn_ssem,
     pn_rsem,
     down_ssem,
@@ -176,7 +178,7 @@
     barrier = pltpu.get_barrier_semaphore()
     partners = [device(lax.rem(place + step, size)) for size, place, device in groups for step in range(1, size)]
     partners += [on_chip(d, core) for k in range(1, FAR_CHIPS + 1) for d in (-k, k)]
-    partners += [on_chip(2 * toward, other)]
+    partners += [on_chip(d * toward, other) for d in (1, 2)]
     for partner in partners:
         pl.semaphore_signal(barrier, inc=1, device_id=partner, device_id_type=MESH)
 
@@ -214,10 +216,11 @@
     for load in loads:
         load.wait()
 
-    for j in range(coup_ref.shape[1]):
-        coup_all[sub, j, :64] = coup_ref[0, j]
-        far_place = far_ref[0, j] - (chip - FAR_CHIPS) * CORES
-        coup_all[sub, j, 64:] = jnp.full((16, 64), far_place.astype(F32), F32).astype(BF16)
+    rank = coup_ref.shape[2]
+    far_base = (chip - FAR_CHIPS) * CORES
+    coup_all[sub, :rank] = jnp.concatenate([coup_ref[0, 0], coup_ref[0, 1]], axis=1)
+    places = jnp.where(lane_half((16, 2 * rank)), far_ref[0, 0] - far_base, far_ref[0, 1] - far_base)
+    coup_all[sub, rank:] = places.astype(F32).astype(BF16)
 
     cols = [split(mm_tn(colt_ref[c], col_ref[c])) for c in range(clusters)]
     rows = [split(mm_tn(rowt_ref[c], row_ref[c])) for c in range(clusters)]
@@ -254,13 +257,14 @@
     def down_copy(step):
         return to_peer(down_send, down_all.at[sub], down_ssem.at[step - 1], down_rsem.at[step - 1], step)
 
-    def pn_copy(step, c):
+    ways = (1, n_sub - 1)
+
+    def mid_copy(c):
+        return to_peer(pn_part.at[c, peer(2)], pn_mid.at[c], mid_sem.at[0, c], mid_sem.at[1, c], ways[c])
+
+    def pn_copy(way, c):
         return to_peer(
-            pn_part.at[c, peer(step)],
-            pn_recv.at[step - 1, c],
-            pn_ssem.at[step - 1, c],
-            pn_rsem.at[step - 1, c],
-            step,
+            pn_part.at[c, peer(ways[way])], pn_recv.at[way, c], pn_ssem.at[way, c], pn_rsem.at[way, c], ways[way]
         )
 
     sides = (1, -1)
@@ -288,11 +292,11 @@
     def ff_copy():
         return remote(far_recv, far_other, ff_sem.at[0], ff_sem.at[1], sibling)
 
-    def ex_copy(e):
-        return remote(ex_send.at[e + 1], ex_recv.at[e + 1], ex_sem.at[0, e + 1], ex_sem.at[1, e + 1], sibling)
+    def ex_copy(i):
+        return remote(ex_send.at[i], ex_recv.at[i], ex_sem.at[0, i], ex_sem.at[1, i], sibling)
 
     def qn_copy(i):
-        device = on_chip(sides[i], core) if i < 2 else on_chip(2 * toward, other)
+        device = (on_chip(toward, core), on_chip(-toward, core), on_chip(toward, other))[i]
         return remote(q_send.at[i], q_recv.at[i], qn_ssem.at[i], qn_rsem.at[i], device)
 
     steps = range(1, n_sub)
@@ -312,12 +316,11 @@
         c_copy(step).wait()
 
     def gather_offset(w, carry):
-        total = jnp.zeros((64, 64), F32)
+        total = jnp.zeros((rank, 2 * rank), F32)
         for s in range(n_sub):
-            for j in range(coup_ref.shape[1]):
-                here = coup_all[s, j, 64:65].astype(F32) == w.astype(F32)
-                total = total + jnp.where(here, coup_all[s, j, :64].astype(F32), 0.0)
-        hi, lo = split(jnp.concatenate([total, total], axis=1))
+            here = coup_all[s, rank : rank + 1].astype(F32) == w.astype(F32)
+            total = total + jnp.where(here, coup_all[s, :rank].astype(F32), 0.0)
+        hi, lo = split(total + jnp.concatenate([total[:, rank:], total[:, :rank]], axis=1))
         cw_hi[w] = hi
         cw_lo[w] = lo
         return carry
@@ -355,34 +358,8 @@
         p_copy(i).wait()
         p_copy(4 + i).start()
 
-    for step in steps:
-        q_copy(step).wait()
     for c in range(clusters):
         tile_copy(c).wait()
-    for c in range(clusters):
-        q_rows = jnp.concatenate([q_all[s, c] for s in range(n_sub)], axis=1)
-
-        def back(k, carry, c=c, q_rows=q_rows):
-            j = c * slots + 2 * k
-            pair = jnp.concatenate([tiles[c, 2 * k], tiles[c, 2 * k + 1]], axis=1)
-            out = mm(q_rows, pair)
-            chain[j] = out[:, :quarter] + chain[table[j]]
-            chain[j + 1] = out[:, quarter:] + chain[table[j + 1]]
-            return carry
-
-        lax.fori_loop(0, slots // 2, back, 0, unroll=slots // 2)
-
-    def back_to(parent, c):
-        return chain[table[at_last + clusters * parent + c]]
-
-    for e in (1, -1, 0):
-        for c in range(clusters):
-            ex_send[e + 1, c] = back_to(near_parent(e, other), c)
-        ex_copy(e).start()
-    for c in range(clusters):
-        q_send[2, c] = back_to(near_parent(2 * toward, other), c)
-    qn_copy(2).start()
-
     for i in range(2, 6):
         p_copy(i).wait()
 
@@ -399,17 +376,41 @@
 
         pn_part[c] = jnp.zeros_like(pn_part[c])
         lax.fori_loop(0, slots // 2, front, 0, unroll=slots // 2)
-        for step in steps:
-            pn_copy(step, c).start()
-
-    near_products(0)
-    for i, e in enumerate(sides):
-        ex_copy(e).wait()
+
+    for c in range(clusters):
+        near_products(c)
+        mid_copy(c).start()
+        pn_copy(1 - c, c).start()
+
+    for step in steps:
+        q_copy(step).wait()
+    for c in range(clusters):
+        q_rows = jnp.concatenate([q_all[s, c] for s in range(n_sub)], axis=1)
+
+        def back(k, carry, c=c, q_rows=q_rows):
+            j = c * slots + 2 * k
+            pair = jnp.concatenate([tiles[c, 2 * k], tiles[c, 2 * k + 1]], axis=1)
+            out = mm(q_rows, pair)
+            chain[j] = out[:, :quarter] + chain[table[j]]
+            chain[j + 1] = out[:, quarter:] + chain[table[j + 1]]
+            return carry
+
+        lax.fori_loop(0, slots // 2, back, 0, unroll=slots // 2)
+
+    def back_to(parent, c):
+        return chain[table[at_last + clusters * parent + c]]
+
+    for c in range(clusters):
+        q_send[2, c] = back_to(near_parent(2 * toward, other), c)
+    qn_copy(2).start()
+    for i, e in ((0, -toward), (2, toward), (1, 0)):
         for c in range(clusters):
-            q_send[i, c] = back_to(near_parent(e, core), c) + ex_recv[e + 1, c]
-        qn_copy(i).start()
-    for c in range(1, clusters):
-        near_products(c)
+            ex_send[i, c] = back_to(near_parent(e, other), c)
+        ex_copy(i).start()
+    ex_copy(0).wait()
+    for c in range(clusters):
+        q_send[0, c] = back_to(near_parent(toward, core), c) + ex_recv[0, c]
+    qn_copy(0).start()
 
     def far_lhs(x):
         hi, lo = split(jnp.where(first, x, 0.0))
@@ -434,6 +435,17 @@
     down_send[...] = jnp.where(first, jnp.concatenate([ph, ph], axis=1), total)
     for step in steps:
         down_copy(step).start()
+    for c in range(clusters):
+        mid_copy(c).wait()
+        pn_part[c, peer(ways[c])] += pn_mid[c]
+        pn_copy(c, c).start()
+    ex_copy(2).wait()
+    for c in range(clusters):
+        q_send[1, c] = back_to(near_parent(-toward, core), c) + ex_recv[2, c]
+    qn_copy(2).wait()
+    for c in range(clusters):
+        q_send[1, c] += q_recv[2, c]
+    qn_copy(1).start()
     down_all[sub] = down_send[...]
     for step in steps:
         down_copy(step).wait()
@@ -443,7 +455,7 @@
     far_hi, far_lo = diagonal(row_hi, col_hi), diagonal(row_lo, col_lo)
     far_field = mm(coeff3, jnp.concatenate([far_hi, far_hi, far_lo], axis=0))
 
-    ex_copy(0).wait()
+    ex_copy(1).wait()
     for c in range(clusters):
         half = 0.5 * mass_ref[c : c + 1]
         t_ref[c] = half * p_ref[c].astype(F32) + far_field[:, c * quarter : (c + 1) * quarter] + pn_part[c, sub]
@@ -451,16 +463,13 @@
         u_ref[c] = u + (back_to(mine, c) + ex_recv[1, c])
 
     for c in range(clusters):
-        for step in steps:
-            pn_copy(step, c).wait()
-        t = t_ref[c]
-        for step in steps:
-            t = t + pn_recv[step - 1, c]
-        t_ref[c] = t
-    for i in range(3):
+        for way in range(2):
+            pn_copy(way, c).wait()
+        t_ref[c] = t_ref[c] + (pn_recv[0, c] + pn_recv[1, c])
+    for i in range(2):
         qn_copy(i).wait()
     for c in range(clusters):
-        u_ref[c] = u_ref[c] + (q_recv[0, c] + q_recv[1, c] + q_recv[2, c])
+        u_ref[c] = u_ref[c] + (q_recv[0, c] + q_recv[1, c])
 
     outs = [
         pltpu.make_async_copy(src, dst, out_sem.at[i]) for i, (src, dst) in enumerate(((t_ref, t_hbm), (u_ref, u_hbm)))
@@ -547,7 +556,7 @@
             pltpu.VMEM(coup.shape, BF16),
             pltpu.VMEM(tiles.shape, BF16),
             pltpu.VMEM((n_sub, *whole), BF16),
-            pltpu.VMEM((n_sub, coup.shape[1], rank + 16, rank), BF16),
+            pltpu.VMEM((n_sub, rank + 16, 2 * rank), BF16),
             pltpu.VMEM((clusters * NEAR_SPAN + 1, rhs, quarter), BF16),
             pltpu.VMEM((rhs, 2 * rank), F32),
             pltpu.VMEM((peers, block, 2 * rank), F32),
@@ -564,7 +573,8 @@
             pltpu.VMEM((3, *whole), F32),
             pltpu.VMEM((3, *whole), F32),
             pltpu.VMEM((clusters, n_sub, rhs, quarter), F32),
-            pltpu.VMEM((peers, *whole), F32),
+            pltpu.VMEM(whole, F32),
+            pltpu.VMEM((2, *whole), F32),
             pltpu.VMEM((block, 2 * rank), F32),
             pltpu.VMEM((n_sub, block, 2 * rank), F32),
             pltpu.VMEM((3, most, 8, rhs), F32),
@@ -586,8 +596,9 @@
             dma((2, 3)),
             dma((3,)),
             dma((3,)),
-            dma((peers, clusters)),
-            dma((peers, clusters)),
+            dma((2, clusters)),
+            dma((2, clusters)),
+            dma((2, clusters)),
             dma((peers,)),
             dma((peers,)),
             dma((3, most)),

time: 61.5 us -> 57.5 us (0.935)
  Pallas kernels: 60.7 us -> 56.5 us
    pallas_call x1, Pallas kernels: 58.7 us -> 54.6 us  [on_device(): pl.pallas_call(functools.partial(kernel, (n_clu, n_sub, n_y)), out_shape=...]
where the time goes in v3:
time: 57.5 us; the launch traced here: 57.1 us
  Pallas kernels  56.5 us (98%)
  between operations  0.64 us (1%)
    pallas_call x1, Pallas kernels, on_device(): pl.pallas_call(functools.partial(kernel, (n_clu, n_sub, n_y)), out_shape=...  54.6 us
    pallas_call x1, Pallas kernels, on_device(): pl.pallas_call(scale_kernel, grid=(clusters,), out_shape=(jax.ShapeDtypeS...  1.95 us

profile of v3, /device:TPU:1, one launch (start us, length us, event | category | flops | bytes accessed | tf_op | source)
XLA Modules:
  0.0 57.1 jit_solution(11070249747847428769)
XLA Ops:
  0.6 54.6 %shard_map.139 = (f32[2,256,128]{2,1,0:T(8,128)}, f32[2,256,128]{2,1,0:T(8,128)}, f32[8,256]{1,0:T(8,128)}) custom-call(s32[2,16]{1,0:T(2,128)} %ids_ref.1, s32[2]{0:T(128)} %count_ref.1, s32[1,2]{1,0:T(1,128)} %far_ref.1, bf16[2,256,128]{2,1,0:T(8,128)(2,1)} %p_hbm.1, bf16[2,256,128]{2,1,0:T(8,128)(2,1)} %q_hbm.1, f32[2,128]{1,0:T(2,128)} %mass_hbm.1, ...), custom_call_target="tpu_custom_call" | custom-call | tf_op jit(solution)/shard_map/pallas_call | solution.py:538
  55.2 1.9 %shard_map.140 = (f32[2,256,128]{2,1,0:T(8,128)}, f32[2,256,128]{2,1,0:T(8,128)}, f32[1,256]{1,0:T(1,128)}) custom-call(f32[8,256]{1,0:T(8,128)} %get-tuple-element.9.scale_ref, f32[2,256,128]{2,1,0:T(8,128)} %get-tuple-element.10.t_ref, f32[2,256,128]{2,1,0:T(8,128)} %get-tuple-element.11.u_ref), custom_call_target="tpu_custom_call" | custom-call | tf_op jit(solution)/shard_map/pallas_call | solution.py:612

commit v4 on v3

--- a/solution.py
+++ b/solution.py
@@ -160,8 +160,8 @@
         pltpu.make_async_copy(src, dst, load_sem.at[i])
         for i, (src, dst) in enumerate(
             (
+                (q_hbm, q_all.at[sub]),
                 (p_hbm, p_ref),
-                (q_hbm, q_all.at[sub]),
                 (col_hbm, col_ref),
                 (row_hbm, row_ref),
                 (colt_hbm, colt_ref),
@@ -175,14 +175,21 @@
     def tile_copy(c):
         return pltpu.make_async_copy(tiles_hbm.at[c], tiles.at[c], tile_sem.at[c])
 
+    for load in loads[:6]:
+        load.start()
+
     barrier = pltpu.get_barrier_semaphore()
-    partners = [device(lax.rem(place + step, size)) for size, place, device in groups for step in range(1, size)]
-    partners += [on_chip(d, core) for k in range(1, FAR_CHIPS + 1) for d in (-k, k)]
-    partners += [on_chip(d * toward, other) for d in (1, 2)]
-    for partner in partners:
+    partners = [
+        (min(step, size - step), device(lax.rem(place + step, size)))
+        for size, place, device in groups
+        for step in range(1, size)
+    ]
+    partners += [(k, on_chip(d, core)) for k in range(1, FAR_CHIPS + 1) for d in (-k, k)]
+    partners += [(d, on_chip(d * toward, other)) for d in (1, 2)]
+    for _, partner in sorted(partners, key=lambda entry: -entry[0]):
         pl.semaphore_signal(barrier, inc=1, device_id=partner, device_id_type=MESH)
 
-    for load in loads:
+    for load in loads[6:]:
         load.start()
     for c in range(clusters):
         tile_copy(c).start()
@@ -244,8 +251,9 @@
     def to_peer(src, dst, ssem, rsem, step):
         return remote(src, dst, ssem, rsem, (clu, peer(step)))
 
-    def q_copy(step):
-        return to_peer(q_all.at[sub], q_all.at[sub], q_ssem.at[step - 1], q_rsem.at[step - 1], step)
+    def q_copy(step, c):
+        own = q_all.at[sub, c]
+        return to_peer(own, own, q_ssem.at[step - 1, c], q_rsem.at[step - 1, c], step)
 
     def c_copy(step):
         return to_peer(coup_all.at[sub], coup_all.at[sub], c_ssem.at[step - 1], c_rsem.at[step - 1], step)
@@ -295,19 +303,21 @@
     def ex_copy(i):
         return remote(ex_send.at[i], ex_recv.at[i], ex_sem.at[0, i], ex_sem.at[1, i], sibling)
 
-    def qn_copy(i):
+    def qn_copy(i, c):
         device = (on_chip(toward, core), on_chip(-toward, core), on_chip(toward, other))[i]
-        return remote(q_send.at[i], q_recv.at[i], qn_ssem.at[i], qn_rsem.at[i], device)
+        return remote(q_send.at[i, c], q_recv.at[i, c], qn_ssem.at[i, c], qn_rsem.at[i, c], device)
 
     steps = range(1, n_sub)
-    for step in steps:
+    far_first = sorted(steps, key=lambda step: -min(step, n_sub - step))
+    for step in far_first:
         up_copy(step).start()
-    for i in range(4):
+    for i in (2, 0, 1, 3):
         p_copy(i).start()
-    for step in steps:
+    for step in far_first:
         c_copy(step).start()
-    for step in steps:
-        q_copy(step).start()
+    for c in range(clusters):
+        for step in far_first:
+            q_copy(step, c).start()
 
     lax.fori_loop(0, n_keys, find, 0)
     lax.fori_loop(0, empty, find_last, 0)
@@ -382,9 +392,9 @@
         mid_copy(c).start()
         pn_copy(1 - c, c).start()
 
-    for step in steps:
-        q_copy(step).wait()
-    for c in range(clusters):
+    for c in range(clusters):
+        for step in steps:
+            q_copy(step, c).wait()
         q_rows = jnp.concatenate([q_all[s, c] for s in range(n_sub)], axis=1)
 
         def back(k, carry, c=c, q_rows=q_rows):
@@ -402,7 +412,7 @@
 
     for c in range(clusters):
         q_send[2, c] = back_to(near_parent(2 * toward, other), c)
-    qn_copy(2).start()
+        qn_copy(2, c).start()
     for i, e in ((0, -toward), (2, toward), (1, 0)):
         for c in range(clusters):
             ex_send[i, c] = back_to(near_parent(e, other), c)
@@ -410,7 +420,7 @@
     ex_copy(0).wait()
     for c in range(clusters):
         q_send[0, c] = back_to(near_parent(toward, core), c) + ex_recv[0, c]
-    qn_copy(0).start()
+        qn_copy(0, c).start()
 
     def far_lhs(x):
         hi, lo = split(jnp.where(first, x, 0.0))
@@ -433,19 +443,19 @@
         ph = ph + mm_nt(far_lhs(far_other[i]), far_rhs(far_parent(-e, other)))
 
     down_send[...] = jnp.where(first, jnp.concatenate([ph, ph], axis=1), total)
-    for step in steps:
+    for step in far_first:
         down_copy(step).start()
+    ex_copy(2).wait()
+    for c in range(clusters):
+        q_send[1, c] = back_to(near_parent(-toward, core), c) + ex_recv[2, c]
+    for c in range(clusters):
+        qn_copy(2, c).wait()
+        q_send[1, c] += q_recv[2, c]
+        qn_copy(1, c).start()
     for c in range(clusters):
         mid_copy(c).wait()
         pn_part[c, peer(ways[c])] += pn_mid[c]
         pn_copy(c, c).start()
-    ex_copy(2).wait()
-    for c in range(clusters):
-        q_send[1, c] = back_to(near_parent(-toward, core), c) + ex_recv[2, c]
-    qn_copy(2).wait()
-    for c in range(clusters):
-        q_send[1, c] += q_recv[2, c]
-    qn_copy(1).start()
     down_all[sub] = down_send[...]
     for step in steps:
         down_copy(step).wait()
@@ -466,9 +476,9 @@
         for way in range(2):
             pn_copy(way, c).wait()
         t_ref[c] = t_ref[c] + (pn_recv[0, c] + pn_recv[1, c])
-    for i in range(2):
-        qn_copy(i).wait()
-    for c in range(clusters):
+    for c in range(clusters):
+        for i in range(2):
+            qn_copy(i, c).wait()
         u_ref[c] = u_ref[c] + (q_recv[0, c] + q_recv[1, c])
 
     outs = [
@@ -480,10 +490,12 @@
     def by_rhs(x):
         return jnp.sum(x.T, axis=0, keepdims=True)
 
+    half_rhs = rhs // 2
     tt = by_rhs(t_ref[0] * t_ref[0] + t_ref[1] * t_ref[1])
     uu = by_rhs(u_ref[0] * u_ref[0] + u_ref[1] * u_ref[1])
     tu = by_rhs(t_ref[0] * u_ref[0] + t_ref[1] * u_ref[1])
-    sums = jnp.concatenate([tt, uu, tu, jnp.zeros((5, rhs), F32)], axis=0)
+    halves = [x[:, k * half_rhs : (k + 1) * half_rhs] for x in (tt, uu, tu) for k in range(2)]
+    sums = jnp.concatenate(halves + [jnp.zeros((2, half_rhs), F32)], axis=0)
     for g, (size, place, device) in enumerate(groups):
         ar[g, place] = sums
 
@@ -505,19 +517,23 @@
         for i in range(1, size):
             sums = sums + ar[g, i]
 
-    rho = 1.0 / jnp.sqrt(sums[0:1] + 1e-06)
-    xi = 1.0 / jnp.sqrt(sums[1:2] + 1e-06)
-    delta = sums[2:3] * (rho * xi)
-    scale_ref[...] = jnp.concatenate([rho, xi, delta, jnp.zeros((5, rhs), F32)], axis=0)
+    rho = 1.0 / jnp.sqrt(sums[0:2] + 1e-06)
+    xi = 1.0 / jnp.sqrt(sums[2:4] + 1e-06)
+    delta = sums[4:6] * (rho * xi)
+    scale_ref[...] = jnp.concatenate([rho, xi, delta, jnp.zeros((2, half_rhs), F32)], axis=0)
     for out in outs:
         out.wait()
 
 
 def scale_kernel(scale_ref, t_ref, u_ref, v_ref, w_ref, delta_ref):
-    rhs, quarter = t_ref.shape[1:]
-    v_ref[0] = t_ref[0] * jnp.broadcast_to(scale_ref[0:1], (quarter, rhs)).T
-    w_ref[0] = u_ref[0] * jnp.broadcast_to(scale_ref[1:2], (quarter, rhs)).T
-    delta_ref[...] = scale_ref[2:3]
+    _, rhs, quarter = t_ref.shape
+    half_rhs = rhs // 2
+    for k, (src, dst) in enumerate(((t_ref, v_ref), (u_ref, w_ref))):
+        for h in range(2):
+            rows = slice(h * half_rhs, (h + 1) * half_rhs)
+            factor = scale_ref[2 * k + h : 2 * k + h + 1]
+            dst[0, rows] = src[0, rows] * jnp.broadcast_to(factor, (quarter, half_rhs)).T
+    delta_ref[...] = jnp.concatenate([scale_ref[4:5], scale_ref[5:6]], axis=1)
 
 
 def on_device(n_y, p_dir, q_dir, mass, tiles, near_ids, near_count, col, row, colt, rowt, coup, far_ids):
@@ -540,7 +556,7 @@
         out_shape=(
             jax.ShapeDtypeStruct(whole, F32),
             jax.ShapeDtypeStruct(whole, F32),
-            jax.ShapeDtypeStruct((8, rhs), F32),
+            jax.ShapeDtypeStruct((8, rhs // 2), F32),
         ),
         in_specs=[smem] * 3 + [hbm] * 9,
         out_specs=(hbm, hbm, vmem),
@@ -577,12 +593,12 @@
             pltpu.VMEM((2, *whole), F32),
             pltpu.VMEM((block, 2 * rank), F32),
             pltpu.VMEM((n_sub, block, 2 * rank), F32),
-            pltpu.VMEM((3, most, 8, rhs), F32),
+            pltpu.VMEM((3, most, 8, rhs // 2), F32),
             dma((2,)),
             dma((8,)),
             dma((clusters,)),
-            dma((peers,)),
-            dma((peers,)),
+            dma((peers, clusters)),
+            dma((peers, clusters)),
             dma((peers,)),
             dma((peers,)),
             dma((6,)),
@@ -594,8 +610,8 @@
             dma((sides,)),
             dma((2,)),
             dma((2, 3)),
-            dma((3,)),
-            dma((3,)),
+            dma((3, clusters)),
+            dma((3, clusters)),
             dma((2, clusters)),
             dma((2, clusters)),
             dma((2, clusters)),
@@ -617,7 +633,7 @@
             jax.ShapeDtypeStruct(whole, F32),
             jax.ShapeDtypeStruct((1, rhs), F32),
         ),
-        in_specs=[pl.BlockSpec((8, rhs), lambda c: (0, 0)), one, one],
+        in_specs=[pl.BlockSpec((8, rhs // 2), lambda c: (0, 0)), one, one],
         out_specs=(one, one, pl.BlockSpec((1, rhs), lambda c: (0, 0))),
         compiler_params=pltpu.CompilerParams(vmem_limit_bytes=VMEM_BYTES),
     )(scale, t, u)

time: 57.5 us -> 56.3 us (0.979)
  Pallas kernels: 56.5 us -> 55.4 us
    pallas_call x1, Pallas kernels: 54.6 us -> 53.5 us  [on_device(): pl.pallas_call(functools.partial(kernel, (n_clu, n_sub, n_y)), out_shape=...]
where the time goes in v4:
time: 56.3 us; the launch traced here: 56.1 us
  Pallas kernels  55.4 us (98%)
  between operations  0.64 us (1%)
    pallas_call x1, Pallas kernels, on_device(): pl.pallas_call(functools.partial(kernel, (n_clu, n_sub, n_y)), out_shape=...  53.5 us
    pallas_call x1, Pallas kernels, on_device(): pl.pallas_call(scale_kernel, grid=(clusters,), out_shape=(jax.ShapeDtypeS...  1.95 us

profile of v4, /device:TPU:1, one launch (start us, length us, event | category | flops | bytes accessed | tf_op | source)
XLA Modules:
  0.0 56.1 jit_solution(16683765216461847772)
XLA Ops:
  0.6 53.5 %shard_map.139 = (f32[2,256,128]{2,1,0:T(8,128)}, f32[2,256,128]{2,1,0:T(8,128)}, f32[8,128]{1,0:T(8,128)}) custom-call(s32[2,16]{1,0:T(2,128)} %ids_ref.1, s32[2]{0:T(128)} %count_ref.1, s32[1,2]{1,0:T(1,128)} %far_ref.1, bf16[2,256,128]{2,1,0:T(8,128)(2,1)} %p_hbm.1, bf16[2,256,128]{2,1,0:T(8,128)(2,1)} %q_hbm.1, f32[2,128]{1,0:T(2,128)} %mass_hbm.1, ...), custom_call_target="tpu_custom_call" | custom-call | tf_op jit(solution)/shard_map/pallas_call | solution.py:554
  54.1 1.9 %shard_map.140 = (f32[2,256,128]{2,1,0:T(8,128)}, f32[2,256,128]{2,1,0:T(8,128)}, f32[1,256]{1,0:T(1,128)}) custom-call(f32[8,128]{1,0:T(8,128)} %get-tuple-element.9.scale_ref, f32[2,256,128]{2,1,0:T(8,128)} %get-tuple-element.10.t_ref, f32[2,256,128]{2,1,0:T(8,128)} %get-tuple-element.11.u_ref), custom_call_target="tpu_custom_call" | custom-call | tf_op jit(solution)/shard_map/pallas_call | solution.py:628

commit v5 on v4

--- a/solution.py
+++ b/solution.py
@@ -310,11 +310,11 @@
     steps = range(1, n_sub)
     far_first = sorted(steps, key=lambda step: -min(step, n_sub - step))
     for step in far_first:
+        c_copy(step).start()
+    for step in far_first:
         up_copy(step).start()
     for i in (2, 0, 1, 3):
         p_copy(i).start()
-    for step in far_first:
-        c_copy(step).start()
     for c in range(clusters):
         for step in far_first:
             q_copy(step, c).start()
@@ -421,6 +421,10 @@
     for c in range(clusters):
         q_send[0, c] = back_to(near_parent(toward, core), c) + ex_recv[0, c]
         qn_copy(0, c).start()
+
+    ex_copy(2).wait()
+    for c in range(clusters):
+        q_send[1, c] = back_to(near_parent(-toward, core), c) + ex_recv[2, c]
 
     def far_lhs(x):
         hi, lo = split(jnp.where(first, x, 0.0))
@@ -445,9 +449,6 @@
     down_send[...] = jnp.where(first, jnp.concatenate([ph, ph], axis=1), total)
     for step in far_first:
         down_copy(step).start()
-    ex_copy(2).wait()
-    for c in range(clusters):
-        q_send[1, c] = back_to(near_parent(-toward, core), c) + ex_recv[2, c]
     for c in range(clusters):
         qn_copy(2, c).wait()
         q_send[1, c] += q_recv[2, c]

time: 56.3 us -> 55.2 us (0.980)
  Pallas kernels: 55.4 us -> 54.4 us
    pallas_call x1, Pallas kernels: 53.5 us -> 52.5 us  [on_device(): pl.pallas_call(functools.partial(kernel, (n_clu, n_sub, n_y)), out_shape=...]
where the time goes in v5:
time: 55.2 us; the launch traced here: 55.1 us
  Pallas kernels  54.4 us (99%)
  between operations  0.64 us (1%)
    pallas_call x1, Pallas kernels, on_device(): pl.pallas_call(functools.partial(kernel, (n_clu, n_sub, n_y)), out_shape=...  52.5 us
    pallas_call x1, Pallas kernels, on_device(): pl.pallas_call(scale_kernel, grid=(clusters,), out_shape=(jax.ShapeDtypeS...  1.95 us

profile of v5, /device:TPU:1, one launch (start us, length us, event | category | flops | bytes accessed | tf_op | source)
XLA Modules:
  0.0 55.1 jit_solution(5656029358430876451)
XLA Ops:
  0.6 52.5 %shard_map.139 = (f32[2,256,128]{2,1,0:T(8,128)}, f32[2,256,128]{2,1,0:T(8,128)}, f32[8,128]{1,0:T(8,128)}) custom-call(s32[2,16]{1,0:T(2,128)} %ids_ref.1, s32[2]{0:T(128)} %count_ref.1, s32[1,2]{1,0:T(1,128)} %far_ref.1, bf16[2,256,128]{2,1,0:T(8,128)(2,1)} %p_hbm.1, bf16[2,256,128]{2,1,0:T(8,128)(2,1)} %q_hbm.1, f32[2,128]{1,0:T(2,128)} %mass_hbm.1, ...), custom_call_target="tpu_custom_call" | custom-call | tf_op jit(solution)/shard_map/pallas_call | solution.py:555
  53.1 1.9 %shard_map.140 = (f32[2,256,128]{2,1,0:T(8,128)}, f32[2,256,128]{2,1,0:T(8,128)}, f32[1,256]{1,0:T(1,128)}) custom-call(f32[8,128]{1,0:T(8,128)} %get-tuple-element.9.scale_ref, f32[2,256,128]{2,1,0:T(8,128)} %get-tuple-element.10.t_ref, f32[2,256,128]{2,1,0:T(8,128)} %get-tuple-element.11.u_ref), custom_call_target="tpu_custom_call" | custom-call | tf_op jit(solution)/shard_map/pallas_call | solution.py:629
